TPU v7x, 128 devices: a whole 4x4x4 slice. The times are simulated.
128 devices in a mesh: section: 2 (over z_lo), dp: 32 (over x, y, core), tensor: 2 (over z_hi).
Axes of the slice: x: 4, y: 4, z: 4 (z_hi: 2, z_lo: 2; z = z_hi * 2 + z_lo), core: 2. Of those that a mesh axis runs over, the one named last changes fastest.
Arguments:
- ends: bfloat16 [2, 2, 32, 192, 1024], P('section', None, 'dp'), may hold values from -6 to 6
- lengths: int32 [2, 32], P(None, 'dp'), may hold values from 48 to 192
- w_qkv: bfloat16 [2, 1024, 3, 1024], P('section', 'dp', None, 'tensor'), may hold values from -0.1875 to 0.1875
- w_out: bfloat16 [2, 1024, 1024], P('section', 'tensor', 'dp'), may hold values from -2 to 2
- w_up: bfloat16 [2, 1024, 4096], P('section', 'dp', 'tensor'), may hold values from -0.1875 to 0.1875
- w_down: bfloat16 [2, 4096, 1024], P('section', 'tensor', 'dp'), may hold values from -0.09375 to 0.09375
- gains: bfloat16 [2, 2, 1024], P('section', None, 'dp'), may hold values from 0.5 to 1.5
- shifts: bfloat16 [2, 4, 1024], P('section', None, 'dp'), may hold values from -1.796875 to 1.796875
- b_qv: bfloat16 [2, 2, 2, 512], P('section', None, 'tensor', 'dp'), may hold values from -1.796875 to 1.796875
- b_ff: bfloat16 [2, 2, 2048], P('section', 'tensor', 'dp'), may hold values from -1.796875 to 1.796875
Outputs:
- ends_out: bfloat16 [2, 2, 32, 192, 1024], P('section', None, 'dp')
- grad_qkv: float32 [2, 1024, 3, 1024], P('section', 'dp', None, 'tensor')
- grad_out: float32 [2, 1024, 1024], P('section', 'tensor', 'dp')
- grad_up: float32 [2, 1024, 4096], P('section', 'dp', 'tensor')
- grad_down: float32 [2, 4096, 1024], P('section', 'tensor', 'dp')
- grad_gains: float32 [2, 2, 1024], P('section', None, 'dp')
- grad_shifts: float32 [2, 4, 1024], P('section', None, 'dp')
- grad_bqv: float32 [2, 2, 2, 512], P('section', None, 'tensor', 'dp')
- grad_bff: float32 [2, 2, 2048], P('section', 'tensor', 'dp')
All inputs are finite; a program needn't handle non-finite values.
Results may differ from a plain program's by a relative error of at most 0.025.
Values may be sent and summed in bfloat16 or wider, within the bound.
A program may use at most 192 MiB of HBM per device.

v0:
```python
import jax
import jax.numpy as jnp
from jax import lax
from jax.experimental import pallas as pl
from jax.experimental.pallas import tpu as pltpu
from jax.sharding import PartitionSpec as P

HD = 64
epsilon = 1e-05

COLS = 6272
MAIN = 6144
ROWS = 192
BLOCK = 512
CHUNKS = ((0, 1536), (1536, 512), (2048, 2048), (4096, 2048))


HALF_A = 3200
OFFSETS = (0, 3, 1, 2)
MESH = pl.DeviceIdType.MESH


def place():
    d = lax.axis_index("dp")
    return lax.div(d, 8), lax.rem(lax.div(d, 2), 4), lax.rem(d, 2), lax.axis_index("tensor")


def dp_at(x, y, c):
    return (x * 4 + y) * 2 + c


def beside(h, phase, step, x, y, c):
    if (h == 0) == (phase == 1):
        return {"dp": dp_at(lax.rem(x + step, 4), y, c)}
    return {"dp": dp_at(x, lax.rem(y + step, 4), c)}


def meet(x, y, c, t):
    barrier = pltpu.get_barrier_semaphore()
    partners = [
        {"dp": dp_at(lax.rem(x + 1, 4), y, c)},
        {"dp": dp_at(lax.rem(x + 3, 4), y, c)},
        {"dp": dp_at(x, lax.rem(y + 1, 4), c)},
        {"dp": dp_at(x, lax.rem(y + 3, 4), c)},
        {"dp": dp_at(x, y, 1 - c)},
        {"tensor": 1 - t},
    ]
    for partner in partners:
        pl.semaphore_signal(barrier, inc=1, device_id=partner, device_id_type=MESH)
    pl.semaphore_wait(barrier, len(partners))


class Sender:
    def __init__(self, send_sems, recv_sems):
        self.send_sems, self.recv_sems, self.copies = send_sems, recv_sems, []

    def __call__(self, src, dst, where):
        i = len(self.copies)
        copy = pltpu.make_async_remote_copy(
            src_ref=src,
            dst_ref=dst,
            send_sem=self.send_sems.at[i],
            recv_sem=self.recv_sems.at[i],
            device_id=where,
            device_id_type=MESH,
        )
        copy.start()
        self.copies.append(copy)
        return copy

    def finish(self):
        for copy in self.copies:
            copy.wait_send()


N_GATHER = 143


def gather_kernel(shard, out, local_sem, send_sems, recv_sems):
    x, y, c, t = place()
    cols = shard.shape[-1]
    part_a, part_b = pl.ds(0, HALF_A), pl.ds(HALF_A, cols - HALF_A)
    meet(x, y, c, t)
    send = Sender(send_sems, recv_sems)
    sibling = {"dp": dp_at(x, y, 1 - c)}
    own = out.at[t, x, y, c]
    local = pltpu.make_async_copy(shard, own, local_sem)
    local.start()
    from_partner = send(shard, own, {"tensor": 1 - t})
    to_sibling = [send(shard, own, sibling)]

    def block(k, h, ja, jb):
        a, b = OFFSETS[ja], OFFSETS[jb]
        dx, dy = (a, b) if h == 0 else (b, a)
        return out.at[t if k == 0 else 1 - t, lax.rem(x + dx, 4), lax.rem(y + dy, 4), c, h]

    def both(k, h, phase, ja):
        dst = block(k, h, ja, 0)
        src = shard.at[h] if (k == 0 and ja == 0) else dst
        return (
            send(src, dst, beside(h, phase, 1, x, y, c)),
            send(src, dst, beside(h, phase, 3, x, y, c)),
        )

    def take(k, h, phase, ja, pair):
        onward = []
        for copy, j, part, step in ((pair[0], 1, part_a, 1), (pair[1], 2, part_b, 3)):
            copy.wait_recv()
            here = block(k, h, *((j, 0) if phase == 1 else (ja, j)))
            onward.append(send(here.at[:, part], here.at[:, part], beside(h, phase, step, x, y, c)))
            to_sibling.append(send(here, here, sibling))
        return onward

    first, second = {}, {}

    def begin(k):
        for h in (0, 1):
            first[k, h] = both(k, h, 1, 0)
        for h in (0, 1):
            second[k, h, 0] = both(k, h, 2, 0)

    begin(0)
    from_partner.wait_recv()
    begin(1)
    mate = out.at[1 - t, x, y, c]
    to_sibling.append(send(mate, mate, sibling))
    for k in (0, 1):
        onward = {}
        for h in (0, 1):
            onward[h] = take(k, h, 1, 0, first[k, h])
        for h in (0, 1):
            for ja in (1, 2):
                second[k, h, ja] = both(k, h, 2, ja)
        for h in (0, 1):
            for copy in onward[h]:
                copy.wait_recv()
            second[k, h, 3] = both(k, h, 2, 3)
            here = block(k, h, 3, 0)
            to_sibling.append(send(here, here, sibling))
        last = []
        for ja in (0, 1, 2, 3):
            for h in (0, 1):
                last.append((h, ja, take(k, h, 2, ja, second[k, h, ja])))
        for h, ja, pair in last:
            for copy in pair:
                copy.wait_recv()
            here = block(k, h, ja, 3)
            to_sibling.append(send(here, here, sibling))
    local.wait()
    for copy in to_sibling:
        copy.wait_recv()
    send.finish()


def gather_weights(shard):
    rows, cols = shard.shape
    out = pl.pallas_call(
        gather_kernel,
        out_shape=jax.ShapeDtypeStruct((2, 4, 4, 2, 2, 16, cols), jnp.bfloat16),
        in_specs=[pl.BlockSpec(memory_space=pl.ANY)],
        out_specs=pl.BlockSpec(memory_space=pl.ANY),
        scratch_shapes=[
            pltpu.SemaphoreType.DMA,
            pltpu.SemaphoreType.DMA((N_GATHER,)),
            pltpu.SemaphoreType.DMA((N_GATHER,)),
        ],
        compiler_params=pltpu.CompilerParams(collective_id=0, has_side_effects=True),
        name="gather_weights",
    )(shard.reshape(2, 16, cols))
    return out.reshape(2, 32 * rows, cols)


N_SCATTER = 65


def scatter_kernel(
    main, extra, out, kept, given, pass_a, pass_b, near_p, near_m, q_a, q_b, q_p, q_m, mine, mate,
    local_sems, send_sems, recv_sems,
):
    x, y, c, t = place()
    cols = kept.shape[-1]
    whole = (pl.ds(0, MAIN), pl.ds(MAIN, cols - MAIN))
    part_a, part_b = pl.ds(0, HALF_A), pl.ds(HALF_A, cols - HALF_A)
    meet(x, y, c, t)
    send = Sender(send_sems, recv_sems)
    sibling = {"dp": dp_at(x, y, 1 - c)}
    f32 = jnp.float32

    def add(dst, *others):
        dst[...] = sum((o[...].astype(f32) for o in others), dst[...].astype(f32)).astype(dst.dtype)

    def half_of(grads, p, h, j, core):
        tt = 1 - t if p == 0 else t
        if h == 0:
            return grads.at[tt, lax.rem(x + OFFSETS[j], 4), :, core, 0]
        return grads.at[tt, :, lax.rem(y + OFFSETS[j], 4), core, 1]

    loads, swaps = {}, {}
    for p in (0, 1):
        for j in (3, 1, 2, 0):
            for h in (0, 1):
                swaps[p, h, j], loads[p, h, j] = [], []
                for grads, part in ((main, whole[0]), (extra, whole[1])):
                    swaps[p, h, j].append(
                        send(half_of(grads, p, h, j, 1 - c), given.at[p, h, j, :, :, part], sibling)
                    )
                    load = pltpu.make_async_copy(
                        half_of(grads, p, h, j, c),
                        kept.at[p, h, j, :, :, part],
                        local_sems.at[len(swaps) * 2 + len(loads[p, h, j]) - 2],
                    )
                    load.start()
                    loads[p, h, j].append(load)

    def settle(p, h, j):
        for load in loads[p, h, j]:
            load.wait()
        for swap in swaps[p, h, j]:
            swap.wait_recv()

    def each(body):
        lax.fori_loop(0, 4, lambda i, z: (body(i), z)[1], 0)

    far, near, q_far, q_near = {}, {}, {}, {}

    def start_far(p):
        for h in (0, 1):
            settle(p, h, 3)
            each(lambda i: add(kept.at[p, h, 3, i], given.at[p, h, 3, i]))
            far[p, h] = (
                send(kept.at[p, h, 3, :, :, part_a], pass_a.at[p, h], beside(h, 1, 1, x, y, c)),
                send(kept.at[p, h, 3, :, :, part_b], pass_b.at[p, h], beside(h, 1, 3, x, y, c)),
            )

    def start_near(p):
        for h in (0, 1):
            settle(p, h, 2)
            settle(p, h, 1)
            far[p, h][0].wait_recv()

            def plus(i):
                add(kept.at[p, h, 2, i, :, part_a], given.at[p, h, 2, i, :, part_a], pass_a.at[p, h, i])
                add(kept.at[p, h, 2, i, :, part_b], given.at[p, h, 2, i, :, part_b])

            each(plus)
            up = send(kept.at[p, h, 2], near_p.at[p, h], beside(h, 1, 1, x, y, c))
            far[p, h][1].wait_recv()

            def minus(i):
                add(kept.at[p, h, 1, i, :, part_b], given.at[p, h, 1, i, :, part_b], pass_b.at[p, h, i])
                add(kept.at[p, h, 1, i, :, part_a], given.at[p, h, 1, i, :, part_a])

            each(minus)
            near[p, h] = (up, send(kept.at[p, h, 1], near_m.at[p, h], beside(h, 1, 3, x, y, c)))

    def line(p, h, j):
        return kept.at[p, h, 0, lax.rem((y if h == 0 else x) + OFFSETS[j], 4)]

    def end_first(p):
        for h in (0, 1):
            settle(p, h, 0)
            for copy in near[p, h]:
                copy.wait_recv()
            each(
                lambda i: add(
                    kept.at[p, h, 0, i], given.at[p, h, 0, i], near_p.at[p, h, i], near_m.at[p, h, i]
                )
            )
            src = line(p, h, 3)
            q_far[p, h] = (
                send(src.at[:, part_a], q_a.at[p, h], beside(h, 2, 1, x, y, c)),
                send(src.at[:, part_b], q_b.at[p, h], beside(h, 2, 3, x, y, c)),
            )

    def mid_second(p):
        for h in (0, 1):
            q_far[p, h][0].wait_recv()
            src = line(p, h, 2)
            add(src.at[:, part_a], q_a.at[p, h])
            up = send(src, q_p.at[p, h], beside(h, 2, 1, x, y, c))
            q_far[p, h][1].wait_recv()
            src = line(p, h, 1)
            add(src.at[:, part_b], q_b.at[p, h])
            q_near[p, h] = (up, send(src, q_m.at[p, h], beside(h, 2, 3, x, y, c)))

    def end_second(p, dst, *more):
        for h in (0, 1):
            for copy in q_near[p, h]:
                copy.wait_recv()
            terms = [line(p, h, 0), q_p.at[p, h], q_m.at[p, h]] + [m.at[h] for m in more]
            dst[h] = sum((o[...].astype(f32) for o in terms[1:]), terms[0][...].astype(f32)).astype(dst.dtype)

    start_far(0)
    start_near(0)
    start_far(1)
    end_first(0)
    start_near(1)
    mid_second(0)
    end_first(1)
    end_second(0, mine)
    across = send(mine, mate, {"tensor": 1 - t})
    mid_second(1)
    across.wait_recv()
    end_second(1, out, mate)
    send.finish()


def scatter_grads(main, extra):
    cols = COLS
    bf = jnp.bfloat16
    rest = cols - HALF_A
    vmem = pltpu.VMEM
    out = pl.pallas_call(
        scatter_kernel,
        out_shape=jax.ShapeDtypeStruct((2, 16, cols), jnp.float32),
        in_specs=[pl.BlockSpec(memory_space=pl.ANY)] * 2,
        out_specs=pl.BlockSpec(memory_space=vmem),
        scratch_shapes=[
            vmem((2, 2, 4, 4, 16, cols), bf),
            vmem((2, 2, 4, 4, 16, cols), bf),
            vmem((2, 2, 4, 16, HALF_A), bf),
            vmem((2, 2, 4, 16, rest), bf),
            vmem((2, 2, 4, 16, cols), bf),
            vmem((2, 2, 4, 16, cols), bf),
            vmem((2, 2, 16, HALF_A), bf),
            vmem((2, 2, 16, rest), bf),
            vmem((2, 2, 16, cols), bf),
            vmem((2, 2, 16, cols), bf),
            vmem((2, 16, cols), bf),
            vmem((2, 16, cols), bf),
            pltpu.SemaphoreType.DMA((32,)),
            pltpu.SemaphoreType.DMA((N_SCATTER,)),
            pltpu.SemaphoreType.DMA((N_SCATTER,)),
        ],
        compiler_params=pltpu.CompilerParams(
            collective_id=1, has_side_effects=True, vmem_limit_bytes=52 * 2**20
        ),
        name="scatter_grads",
    )(main.reshape(2, 4, 4, 2, 2, 16, MAIN), extra.reshape(2, 4, 4, 2, 2, 16, cols - MAIN))
    return out.reshape(32, cols)


def dot(a, b):
    return lax.dot_general(a, b, (((1,), (0,)), ((), ())), preferred_element_type=jnp.float32)


def dot_nt(a, b):
    return lax.dot_general(a, b, (((1,), (1,)), ((), ())), preferred_element_type=jnp.float32)


def dot_tn(a, b):
    return lax.dot_general(a, b, (((0,), (0,)), ((), ())), preferred_element_type=jnp.float32)


def low(v):
    return v.astype(jnp.bfloat16)


def high(v):
    return v.astype(jnp.float32)


def columns(start, size):
    return pl.ds(pl.multiple_of(start, 128), size)


def each(count, work):
    lax.fori_loop(0, count, lambda i, z: (work(i), z)[1], 0)


def total(v):
    return jnp.sum(v, axis=0, keepdims=True)


def normalize(values):
    centred = values - jnp.mean(values, -1, keepdims=True)
    inverse_std = lax.rsqrt(jnp.mean(centred * centred, -1, keepdims=True) + epsilon)
    return centred * inverse_std, inverse_std


def norm_backward(grad_norm, normed, inverse_std):
    return inverse_std * (
        grad_norm
        - jnp.mean(grad_norm, -1, keepdims=True)
        - normed * jnp.mean(grad_norm * normed, -1, keepdims=True)
    )


def layers_kernel(
    lengths, ends, full, gains, shifts, b_qv, b_ff,
    ends_out, grads, d_gains, d_shifts, d_bqv, d_bff,
    w, x_own, x_in, relay, q, k, v, o, probs, n1, n2, i1, i2, res, hid, act, slope, d_act, d_qkv,
    acc, d_low, a_low, kept, stage,
    load_sems, io_sems, stage_sems, send_sems, recv_sems,
):
    s, t = lax.axis_index("section"), lax.axis_index("tensor")
    loads = {}
    own_load = pltpu.make_async_copy(ends.at[t], x_own, io_sems.at[0])
    own_load.start()
    for n, (start, size) in enumerate(CHUNKS):
        for half in (0, 1):
            part = pl.ds(start, size)
            load = pltpu.make_async_copy(
                full.at[half, :, part], w.at[half, :, part], load_sems.at[2 * n + half]
            )
            load.start()
            loads[n, half] = load

    barrier = pltpu.get_barrier_semaphore()
    pl.semaphore_signal(barrier, inc=1, device_id={"section": 1 - s}, device_id_type=MESH)
    pl.semaphore_signal(barrier, inc=1, device_id={"tensor": 1 - t}, device_id_type=MESH)
    pl.semaphore_wait(barrier, 2)

    def ready(n):
        for half in (0, 1):
            if (n, half) in loads:
                loads.pop((n, half)).wait()

    length = lengths[t, 0]
    first_half = lax.broadcasted_iota(jnp.int32, (ROWS, 128), 1) < HD
    valid = lax.broadcasted_iota(jnp.int32, (ROWS, ROWS), 1) < length
    scale = HD**-0.5

    def pick(e, value):
        return jnp.where(first_half == (e == 0), value, jnp.zeros_like(value))

    def forward(x):
        ready(0)

        def project(i):
            half, j = lax.div(i, 3), lax.rem(i, 3)
            p = dot(x[...], w[half, :, columns(j * BLOCK, BLOCK)])
            at = columns(half * BLOCK, BLOCK)

            @pl.when(j == 0)
            def _():
                q[:, at] = low(p + b_qv[0:1, at])

            @pl.when(j == 1)
            def _():
                k[:, at] = low(p)

            @pl.when(j == 2)
            def _():
                v[:, at] = low(p + b_qv[1:2, at])

        each(6, project)

        def heads(i):
            at = columns(i * 128, 128)
            kp, vp, qp = k[:, at], v[:, at], q[:, at]
            outs = []
            for e in (0, 1):
                scores = dot_nt(pick(e, qp), kp) * scale
                scores = jnp.where(valid, scores, -1e9)
                powers = jnp.exp(scores - jnp.max(scores, -1, keepdims=True))
                p = powers / jnp.sum(powers, -1, keepdims=True)
                probs[2 * i + e] = p
                outs.append(dot(low(p), vp))
            o[:, at] = low(jnp.where(first_half, outs[0], outs[1]))

        each(8, heads)
        ready(1)
        attended = dot_nt(o[:, 0:512], w[0, :, 1536:2048]) + dot_nt(o[:, 512:1024], w[1, :, 1536:2048])
        normed, inverse = normalize(high(x[...]) + attended + shifts[0:1])
        n1[...], i1[...] = normed, inverse
        hidden = normed * gains[0:1] + shifts[1:2]
        res[...] = hidden
        hid[...] = low(hidden)
        ready(2)

        def widen(i):
            half, j = lax.div(i, 4), lax.rem(i, 4)
            at = columns(i * BLOCK, BLOCK)
            u = dot(hid[...], w[half, :, columns(2048 + j * BLOCK, BLOCK)]) + b_ff[:, at]
            phi = 0.5 + 0.5 * lax.erf(u * 0.7071067811865476)
            act[:, at] = low(u * phi)
            slope[:, at] = phi + u * (jnp.exp(u * u * -0.5) * 0.3989422804014327)

        each(8, widen)
        ready(3)

        def narrow(i):
            at = columns(i * 256, 256)
            rows = pl.ds(pl.multiple_of(i * 256, 256), 256)
            acc[:, at] = dot_nt(act[:, 0:2048], w[0, rows, 4096:6144]) + dot_nt(
                act[:, 2048:4096], w[1, rows, 4096:6144]
            )

        each(4, narrow)
        normed, inverse = normalize(res[...] + acc[...] + shifts[2:3])
        n2[...], i2[...] = normed, inverse
        return low(normed * gains[1:2] + shifts[3:4])

    def backward(grad_out):
        normed = n2[...]
        d_gains[1:2] = total(grad_out * normed)
        d_shifts[3:4] = total(grad_out)
        d_sum = norm_backward(grad_out * gains[1:2], normed, i2[...])
        d_shifts[2:3] = total(d_sum)
        res[...] = d_sum
        d_low[...] = low(d_sum)

        def widen(i):
            half, j = lax.div(i, 4), lax.rem(i, 4)
            at = columns(i * BLOCK, BLOCK)
            d = low(dot(d_low[...], w[half, :, columns(4096 + j * BLOCK, BLOCK)]) * slope[:, at])
            d_act[:, at] = d
            d_bff[:, at] = total(high(d))

        each(8, widen)

        def narrow(i):
            at = columns(i * 256, 256)
            rows = pl.ds(pl.multiple_of(i * 256, 256), 256)
            acc[:, at] = dot_nt(d_act[:, 0:2048], w[0, rows, 2048:4096]) + dot_nt(
                d_act[:, 2048:4096], w[1, rows, 2048:4096]
            )

        each(4, narrow)
        d_hidden = res[...] + acc[...]
        normed = n1[...]
        d_gains[0:1] = total(d_hidden * normed)
        d_shifts[1:2] = total(d_hidden)
        d_sum = norm_backward(d_hidden * gains[0:1], normed, i1[...])
        d_shifts[0:1] = total(d_sum)
        res[...] = d_sum
        a_low[...] = low(d_sum)

        def heads(i):
            at = columns(i * 128, 128)
            half = lax.div(i, 4)
            d_o = low(dot(a_low[...], w[half, :, columns(1536 + lax.rem(i, 4) * 128, 128)]))
            kp, vp, qp = k[:, at], v[:, at], q[:, at]
            parts = []
            for e in (0, 1):
                p = probs[2 * i + e]
                d_p = dot_nt(pick(e, d_o), vp)
                d_s = low(p * (d_p - jnp.sum(p * d_p, -1, keepdims=True)))
                parts.append((dot(d_s, kp) * scale, dot_tn(d_s, qp) * scale, dot_tn(low(p), d_o)))
            d_q, d_k, d_v = (low(jnp.where(first_half, a, b)) for a, b in zip(*parts))
            d_qkv[0, :, at] = d_q
            d_qkv[1, :, at] = d_k
            d_qkv[2, :, at] = d_v
            d_bqv[0:1, at] = total(high(d_q))
            d_bqv[1:2, at] = total(high(d_v))

        each(8, heads)

        def narrow_in(i):
            at = columns(i * 256, 256)
            rows = pl.ds(pl.multiple_of(i * 256, 256), 256)
            acc[:, at] = sum(
                dot_nt(d_qkv[j, :, 512 * half : 512 * half + 512], w[half, rows, 512 * j : 512 * j + 512])
                for half in (0, 1)
                for j in (0, 1, 2)
            )

        each(4, narrow_in)
        return low(res[...] + acc[...])

    def weight_grads(x):
        def block(i, half, start, left, right):
            slot = lax.rem(i, 4)
            copy = pltpu.make_async_copy(
                stage.at[slot], grads.at[half, :, columns(start, BLOCK)], stage_sems.at[slot]
            )

            @pl.when(i >= 4)
            def _():
                copy.wait()

            stage[slot] = low(dot_tn(left, right))
            copy.start()

        def narrow(i):
            block(i, lax.div(i, 4), 4096 + lax.rem(i, 4) * BLOCK, d_low[...], act[:, columns(i * BLOCK, BLOCK)])

        def widen(i):
            block(i + 8, lax.div(i, 4), 2048 + lax.rem(i, 4) * BLOCK, hid[...], d_act[:, columns(i * BLOCK, BLOCK)])

        def attend(i):
            block(i + 16, i, 1536, a_low[...], o[:, columns(i * BLOCK, BLOCK)])

        def project(i):
            half, j = lax.div(i, 3), lax.rem(i, 3)
            block(i + 18, half, j * BLOCK, x[...], d_qkv[j, :, columns(half * BLOCK, BLOCK)])

        each(8, narrow)
        each(8, widen)
        each(2, attend)
        each(6, project)
        for slot in range(4):
            pltpu.make_async_copy(
                stage.at[slot], grads.at[0, :, pl.ds(0, BLOCK)], stage_sems.at[slot]
            ).wait()

    def exchange(n):
        copy = pltpu.make_async_remote_copy(
            src_ref=kept.at[n],
            dst_ref=relay.at[n],
            send_sem=send_sems.at[n],
            recv_sem=recv_sems.at[n],
            device_id={"section": 1 - s},
            device_id_type=MESH,
        )
        copy.start()
        copy.wait()
        return relay[n]

    own_load.wait()
    kept[0] = forward(x_own)
    x_in[...] = jnp.where(s == 0, x_own[...], exchange(0))
    result = forward(x_in)
    kept[2] = result
    kept[1] = backward(high(x_own[...]))
    grad_out = jnp.where(s == 1, x_own[...], exchange(1))
    d_x = backward(high(grad_out))
    kept[2] = jnp.where(s == 0, d_x, kept[2])
    across = pltpu.make_async_remote_copy(
        src_ref=kept.at[2],
        dst_ref=ends_out.at[t],
        send_sem=send_sems.at[2],
        recv_sem=recv_sems.at[2],
        device_id={"tensor": 1 - t},
        device_id_type=MESH,
    )
    across.start()
    here = pltpu.make_async_copy(kept.at[2], ends_out.at[t], io_sems.at[1])
    here.start()
    weight_grads(x_in)
    here.wait()
    across.wait()


def run_layers(lengths, ends, full, gains, shifts, b_qv, b_ff):
    vmem = pltpu.VMEM
    bf, f32 = jnp.bfloat16, jnp.float32
    hbm = pl.BlockSpec(memory_space=pl.ANY)
    near = pl.BlockSpec(memory_space=vmem)
    sem = pltpu.SemaphoreType.DMA
    shape = jax.ShapeDtypeStruct
    return pl.pallas_call(
        layers_kernel,
        out_shape=(
            shape((2, ROWS, 1024), bf),
            shape((2, 1024, MAIN), bf),
            shape((2, 1024), f32),
            shape((4, 1024), f32),
            shape((2, 1024), f32),
            shape((1, 4096), f32),
        ),
        in_specs=[pl.BlockSpec(memory_space=pltpu.SMEM), hbm, hbm, near, near, near, near],
        out_specs=(hbm, hbm, near, near, near, near),
        scratch_shapes=[
            vmem((2, 1024, MAIN), bf),
            vmem((ROWS, 1024), bf),
            vmem((ROWS, 1024), bf),
            vmem((2, ROWS, 1024), bf),
            vmem((ROWS, 1024), bf),
            vmem((ROWS, 1024), bf),
            vmem((ROWS, 1024), bf),
            vmem((ROWS, 1024), bf),
            vmem((16, ROWS, ROWS), f32),
            vmem((ROWS, 1024), f32),
            vmem((ROWS, 1024), f32),
            vmem((ROWS, 1), f32),
            vmem((ROWS, 1), f32),
            vmem((ROWS, 1024), f32),
            vmem((ROWS, 1024), bf),
            vmem((ROWS, 4096), bf),
            vmem((ROWS, 4096), f32),
            vmem((ROWS, 4096), bf),
            vmem((3, ROWS, 1024), bf),
            vmem((ROWS, 1024), f32),
            vmem((ROWS, 1024), bf),
            vmem((ROWS, 1024), bf),
            vmem((3, ROWS, 1024), bf),
            vmem((4, 1024, BLOCK), bf),
            sem((8,)),
            sem((2,)),
            sem((4,)),
            sem((3,)),
            sem((3,)),
        ],
        compiler_params=pltpu.CompilerParams(
            collective_id=2, has_side_effects=True, vmem_limit_bytes=58 * 2**20
        ),
        name="run_layers",
    )(lengths, ends, full, gains, shifts, b_qv, b_ff)


def pack_shard(w_qkv, w_out, w_up, w_down, gains, shifts, b_qv, b_ff):
    extra = jnp.concatenate(
        [gains[0].T, shifts[0].T, b_qv[0, :, 0].reshape(32, 1), b_ff[0, 0].reshape(2, 32).T], axis=1
    )
    return jnp.concatenate(
        [
            w_qkv[0].reshape(32, 1536),
            w_out[0].T,
            w_up[0],
            w_down[0].T,
            jnp.pad(extra, ((0, 0), (0, 119))),
        ],
        axis=1,
    )


def unpack_extra(extra):
    extra = extra.astype(jnp.float32)
    gains = extra[0, :, 0:2].T
    shifts = extra[0, :, 2:6].T
    b_qv = extra[:, :, 6].reshape(2, 32, 2, 16).transpose(2, 0, 1, 3).reshape(2, 1024)
    b_ff = extra[:, :, 7:9].reshape(2, 32, 32, 2).transpose(0, 1, 3, 2).reshape(4096)
    return gains, shifts, b_qv, b_ff


def pack_extra(gains, shifts, b_qv, b_ff):
    common = jnp.concatenate([gains, shifts], axis=0).T
    return jnp.concatenate(
        [
            jnp.broadcast_to(common, (2, 1024, 6)),
            b_qv.reshape(2, 2, 32, 16).transpose(1, 2, 0, 3).reshape(2, 1024, 1),
            b_ff.reshape(2, 32, 2, 32).transpose(0, 1, 3, 2).reshape(2, 1024, 2),
            jnp.zeros((2, 1024, 119), gains.dtype),
        ],
        axis=2,
    )


def unpack_shard(got):
    extra = got[:, 6144:]
    return (
        got[:, :1536].reshape(1, 32, 3, 512),
        got[:, 1536:2048].T[None],
        got[:, 2048:4096][None],
        got[:, 4096:6144].T[None],
        extra[:, 0:2].T[None],
        extra[:, 2:6].T[None],
        extra[:, 6].reshape(1, 2, 1, 16),
        extra[:, 7:9].T.reshape(1, 1, 64),
    )


def body(ends, lengths, w_qkv, w_out, w_up, w_down, gains, shifts, b_qv, b_ff):
    full = gather_weights(pack_shard(w_qkv, w_out, w_up, w_down, gains, shifts, b_qv, b_ff))
    gains, shifts, b_qv, b_ff = unpack_extra(full[:, :, MAIN:])
    ends_out, main, d_gains, d_shifts, d_bqv, d_bff = run_layers(
        lengths, ends.reshape(2, ROWS, 1024), full, gains, shifts, b_qv, b_ff.reshape(1, 4096)
    )
    extra = pack_extra(d_gains, d_shifts, d_bqv, d_bff.reshape(4096)).astype(jnp.bfloat16)
    return (ends_out.reshape(1, 2, 1, ROWS, 1024),) + unpack_shard(scatter_grads(main, extra))


def solution(mesh):
    in_specs = (
        P("section", None, "dp", None, None),
        P(None, "dp"),
        P("section", "dp", None, "tensor"),
        P("section", "tensor", "dp"),
        P("section", "dp", "tensor"),
        P("section", "tensor", "dp"),
        P("section", None, "dp"),
        P("section", None, "dp"),
        P("section", None, "tensor", "dp"),
        P("section", "tensor", "dp"),
    )
    out_specs = (
        P("section", None, "dp", None, None),
        P("section", "dp", None, "tensor"),
        P("section", "tensor", "dp"),
        P("section", "dp", "tensor"),
        P("section", "tensor", "dp"),
        P("section", None, "dp"),
        P("section", None, "dp"),
        P("section", None, "tensor", "dp"),
        P("section", "tensor", "dp"),
    )
    return jax.shard_map(body, mesh=mesh, in_specs=in_specs, out_specs=out_specs, check_vma=False)
```

profile of v0, /device:TPU:1, one launch (start us, length us, event | category | flops | bytes accessed | tf_op | source)
XLA Modules:
  0.0 302.0 jit_solution(4027393765666598936)
XLA Ops:
  0.6 0.0 copy-start.2
  0.7 1.0 copy.34
  1.6 0.1 concatenate.29
  1.8 0.8 constant_dynamic-update-slice_fusion.3
  2.6 0.9 constant_dynamic-update-slice_fusion.2
  3.5 0.9 constant_dynamic-update-slice_fusion.1
  4.4 0.5 broadcast.15
  4.9 1.3 reduce.9
  6.2 0.1 reshape_squeeze.14
  6.3 0.7 reshape_squeeze.13
  7.1 0.7 pad_maximum_fusion
  7.8 0.1 copy.54
  7.9 0.0 copy-start.1
  7.9 0.7 copy-done.1
  8.6 82.0 %gather_weights.1 = bf16[2,4,4,2,2,16,6272]{6,5,4,3,2,1,0:T(8,128)(2,1)} custom-call(bf16[2,16,6272]{2,1,0:T(8,128)(2,1)} %copy-done.1), custom_call_target="tpu_custom_call" | custom-call | tf_op jit(solution)/shard_map/gather_weights/pallas_call | solution.py:157
  90.7 1.1 slice.57
  91.8 0.2 copy.53
  92.0 0.1 convert_element_type.7
  92.1 0.1 reshape_squeeze.15
  92.3 0.7 reshape.71.b_qv
  93.0 0.6 slice_bitcast_fusion.6.shifts
  93.6 0.6 slice_bitcast_fusion.7.gains
  94.2 0.1 reshape.72
  94.3 0.1 copy.56
  94.4 0.7 reshape_reshape.7.b_ff
  95.1 0.0 copy-done.2
  95.1 0.6 copy.39.lengths
  95.8 116.5 %run_layers.1 = (bf16[2,192,1024]{2,1,0:T(8,128)(2,1)}, bf16[2,1024,6144]{2,1,0:T(8,128)(2,1)}, f32[2,1024]{1,0:T(2,128)}, f32[4,1024]{1,0:T(4,128)}, f32[2,1024]{1,0:T(2,128)}, /*index=5*/f32[1,4096]{1,0:T(1,128)}) custom-call(s32[2,1]{1,0:T(2,128)} %copy.39.lengths, bf16[2,192,1024]{2,1,0:T(8,128)(2,1)} %bitcast.83, bf16[2,1024,6272]{2,1,0:T(8,128)(2,1)} %bitcast.79, ...), custom_call_target="tpu_custom_call" | custom-call | tf_op jit(solution)/shard_map/run_layers/pallas_call | solution.py:643
  212.2 0.0 copy-start
  212.2 0.8 fusion
  213.1 0.2 copy.50
  213.3 0.1 broadcast_in_dim.24
  213.4 0.8 convert_reduce_fusion
  214.2 0.1 reshape_reshape.8
  214.3 0.5 copy.42
  214.8 0.7 convert.19
  215.5 0.1 reshape.75
  215.6 0.8 copy.43
  216.4 0.1 pad.8.clone
  216.5 0.5 maximum_maximum_fusion.extra
  217.0 78.7 %scatter_grads.1 = f32[2,16,6272]{2,1,0:T(8,128)S(1)} custom-call(bf16[2,4,4,2,2,16,6144]{6,5,4,3,2,1,0:T(8,128)(2,1)} %bitcast.80, bf16[2,4,4,2,2,16,128]{6,5,4,3,2,1,0:T(8,128)(2,1)S(1)} %maximum_maximum_fusion.extra), custom_call_target="tpu_custom_call" | custom-call | tf_op jit(solution)/shard_map/scatter_grads/pallas_call | solution.py:313
  295.8 0.1 reshape.77
  295.9 0.7 copy.48
  296.7 0.8 slice_bitcast_fusion
  297.5 0.6 slice_bitcast_fusion.2
  298.1 0.1 slice_bitcast_fusion.3
  298.2 0.1 copy.46
  298.3 0.6 reshape.78
  298.9 0.6 copy.44
  299.5 0.1 slice_bitcast_fusion.4
  299.6 0.7 copy.45
  300.2 0.2 slice_reduce_fusion
  300.4 0.7 reshape_squeeze.16
  301.1 0.0 copy-done
  301.1 0.9 copy.62
  (8 shorter events, 0.1 us)
Async XLA Ops:
  0.6 94.5 %copy-start.2 = (s32[2,1]{0,1:T(1,128)S(1)}, s32[2,1]{0,1:T(1,128)}, u32[]{:S(2)}) copy-start(s32[2,1]{0,1:T(1,128)} %param.11) | copy-start | bytes 28
  7.9 0.8 copy-start.1
  212.2 88.8 %copy-start = (bf16[2,192,1024]{2,1,0:T(8,128)(2,1)S(1)}, bf16[2,192,1024]{2,1,0:T(8,128)(2,1)}, u32[]{:S(2)}) copy-start(bf16[2,192,1024]{2,1,0:T(8,128)(2,1)} %get-tuple-element.15) | copy-start | bytes 2359300
where the time goes:
time: 304 us; the launch traced here: 302 us
  Pallas kernels  277 us (91%)
  local copies, waits for them, and re-layouts  19 us (6%)
  other arithmetic  4.91 us (2%)
    pallas_call x1, Pallas kernels, run_layers(): pl.pallas_call(layers_kernel, out_shape=(shape((2, ROWS, 1024), bf), shap...  116 us
    pallas_call x1, Pallas kernels, gather_weights(): pl.pallas_call(gather_kernel, out_shape=jax.ShapeDtypeStruct((2, 4, 4, 2,...  82 us
    pallas_call x1, Pallas kernels, scatter_grads(): pl.pallas_call(scatter_kernel, out_shape=jax.ShapeDtypeStruct((2, 16, col...  78.7 us
    unnamed x17, local copies, waits for them, and re-layouts  7.43 us

commit v1 on v0

v1 whole, which is shorter than its diff:
```python
import jax
import jax.numpy as jnp
from jax import lax
from jax.experimental import pallas as pl
from jax.experimental.pallas import tpu as pltpu
from jax.sharding import PartitionSpec as P

HD = 64
epsilon = 1e-05

COLS = 6272
ROWS = 192
BLOCK = 512
EXTRA, UP, DOWN = 2048, 2176, 4224
CHUNKS = ((0, 1536), (1536, 512), (UP, 2048), (DOWN, 2048))
PASSES = ((DOWN, 2048, 1024), (UP, 2048, 1024), (0, 2176, 1152))


HALF_A = 3200
OFFSETS = (0, 3, 1, 2)
MESH = pl.DeviceIdType.MESH


def place():
    d = lax.axis_index("dp")
    return lax.div(d, 8), lax.rem(lax.div(d, 2), 4), lax.rem(d, 2), lax.axis_index("tensor")


def dp_at(x, y, c):
    return (x * 4 + y) * 2 + c


def beside(h, phase, step, x, y, c):
    if (h == 0) == (phase == 1):
        return {"dp": dp_at(lax.rem(x + step, 4), y, c)}
    return {"dp": dp_at(x, lax.rem(y + step, 4), c)}


def meet(x, y, c, t):
    barrier = pltpu.get_barrier_semaphore()
    partners = [
        {"dp": dp_at(lax.rem(x + 1, 4), y, c)},
        {"dp": dp_at(lax.rem(x + 3, 4), y, c)},
        {"dp": dp_at(x, lax.rem(y + 1, 4), c)},
        {"dp": dp_at(x, lax.rem(y + 3, 4), c)},
        {"dp": dp_at(x, y, 1 - c)},
        {"tensor": 1 - t},
        {"section": 1 - lax.axis_index("section")},
    ]
    for partner in partners:
        pl.semaphore_signal(barrier, inc=1, device_id=partner, device_id_type=MESH)
    pl.semaphore_wait(barrier, len(partners))


class Sender:
    def __init__(self, send_sems, recv_sems):
        self.send_sems, self.recv_sems, self.copies = send_sems, recv_sems, []

    def __call__(self, src, dst, where):
        i = len(self.copies)
        copy = pltpu.make_async_remote_copy(
            src_ref=src,
            dst_ref=dst,
            send_sem=self.send_sems.at[i],
            recv_sem=self.recv_sems.at[i],
            device_id=where,
            device_id_type=MESH,
        )
        copy.start()
        self.copies.append(copy)
        return copy

    def finish(self):
        for copy in self.copies:
            copy.wait_send()


N_GATHER = 143


def gather_kernel(shard, out, local_sem, send_sems, recv_sems):
    x, y, c, t = place()
    cols = shard.shape[-1]
    part_a, part_b = pl.ds(0, HALF_A), pl.ds(HALF_A, cols - HALF_A)
    meet(x, y, c, t)
    send = Sender(send_sems, recv_sems)
    sibling = {"dp": dp_at(x, y, 1 - c)}
    own = out.at[t, x, y, c]
    local = pltpu.make_async_copy(shard, own, local_sem)
    local.start()
    from_partner = send(shard, own, {"tensor": 1 - t})
    to_sibling = [send(shard, own, sibling)]

    def block(k, h, ja, jb):
        a, b = OFFSETS[ja], OFFSETS[jb]
        dx, dy = (a, b) if h == 0 else (b, a)
        return out.at[t if k == 0 else 1 - t, lax.rem(x + dx, 4), lax.rem(y + dy, 4), c, h]

    def both(k, h, phase, ja):
        dst = block(k, h, ja, 0)
        src = shard.at[h] if (k == 0 and ja == 0) else dst
        return (
            send(src, dst, beside(h, phase, 1, x, y, c)),
            send(src, dst, beside(h, phase, 3, x, y, c)),
        )

    def take(k, h, phase, ja, pair):
        onward = []
        for copy, j, part, step in ((pair[0], 1, part_a, 1), (pair[1], 2, part_b, 3)):
            copy.wait_recv()
            here = block(k, h, *((j, 0) if phase == 1 else (ja, j)))
            onward.append(send(here.at[:, part], here.at[:, part], beside(h, phase, step, x, y, c)))
            to_sibling.append(send(here, here, sibling))
        return onward

    first, second = {}, {}

    def begin(k):
        for h in (0, 1):
            first[k, h] = both(k, h, 1, 0)
        for h in (0, 1):
            second[k, h, 0] = both(k, h, 2, 0)

    mate = out.at[1 - t, x, y, c]
    onward, last = {}, {}

    def first_in(k):
        for h in (0, 1):
            onward[k, h] = take(k, h, 1, 0, first[k, h])
        for h in (0, 1):
            for ja in (1, 2):
                second[k, h, ja] = both(k, h, 2, ja)

    def far_in(k):
        for h in (0, 1):
            for copy in onward[k, h]:
                copy.wait_recv()
            second[k, h, 3] = both(k, h, 2, 3)
            here = block(k, h, 3, 0)
            to_sibling.append(send(here, here, sibling))

    def second_in(k, *places):
        for ja in places:
            for h in (0, 1):
                last[k, h, ja] = take(k, h, 2, ja, second[k, h, ja])

    def last_in(k):
        for ja in (0, 1, 2, 3):
            for h in (0, 1):
                for copy in last[k, h, ja]:
                    copy.wait_recv()
                here = block(k, h, ja, 3)
                to_sibling.append(send(here, here, sibling))

    begin(0)
    first_in(0)
    from_partner.wait_recv()
    begin(1)
    to_sibling.append(send(mate, mate, sibling))
    far_in(0)
    second_in(0, 0)
    first_in(1)
    second_in(0, 1, 2)
    far_in(1)
    second_in(1, 0)
    second_in(0, 3)
    second_in(1, 1, 2)
    last_in(0)
    second_in(1, 3)
    last_in(1)
    local.wait()
    for copy in to_sibling:
        copy.wait_recv()
    send.finish()


def gather_weights(shard):
    rows, cols = shard.shape
    out = pl.pallas_call(
        gather_kernel,
        out_shape=jax.ShapeDtypeStruct((2, 4, 4, 2, 2, 16, cols), jnp.bfloat16),
        in_specs=[pl.BlockSpec(memory_space=pl.ANY)],
        out_specs=pl.BlockSpec(memory_space=pl.ANY),
        scratch_shapes=[
            pltpu.SemaphoreType.DMA,
            pltpu.SemaphoreType.DMA((N_GATHER,)),
            pltpu.SemaphoreType.DMA((N_GATHER,)),
        ],
        compiler_params=pltpu.CompilerParams(collective_id=0, has_side_effects=True),
        name="gather_weights",
    )(shard.reshape(2, 16, cols))
    return out.reshape(2, 32 * rows, cols)


N_EACH = 60


def dot(a, b):
    return lax.dot_general(a, b, (((1,), (0,)), ((), ())), preferred_element_type=jnp.float32)


def dot_nt(a, b):
    return lax.dot_general(a, b, (((1,), (1,)), ((), ())), preferred_element_type=jnp.float32)


def dot_tn(a, b):
    return lax.dot_general(a, b, (((0,), (0,)), ((), ())), preferred_element_type=jnp.float32)


def low(v):
    return v.astype(jnp.bfloat16)


def high(v):
    return v.astype(jnp.float32)


def columns(start, size):
    return pl.ds(pl.multiple_of(start, 128), size)


def each(count, work):
    lax.fori_loop(0, count, lambda i, z: (work(i), z)[1], 0)


def total(v):
    return jnp.sum(v, axis=0, keepdims=True)


def normalize(values):
    centred = values - jnp.mean(values, -1, keepdims=True)
    inverse_std = lax.rsqrt(jnp.mean(centred * centred, -1, keepdims=True) + epsilon)
    return centred * inverse_std, inverse_std


def norm_backward(grad_norm, normed, inverse_std):
    return inverse_std * (
        grad_norm
        - jnp.mean(grad_norm, -1, keepdims=True)
        - normed * jnp.mean(grad_norm * normed, -1, keepdims=True)
    )


def layers_kernel(
    lengths, ends, full, gains, shifts, b_qv, b_ff,
    ends_out, out,
    d_gains, d_shifts, d_bqv, d_bff,
    w, x_own, x_in, relay, q, k, v, o, probs, n1, n2, i1, i2, res, hid, act, slope, d_act, d_qkv,
    acc, d_low, a_low, kept, small,
    s_x, s_hid, s_d_low, s_a_low, s_act, s_d_act, s_o, s_d_qkv, s_small,
    passing, near_p, near_m, q_passing, q_p, q_m, mate, to_mate,
    load_sems, io_sems, send_sems, recv_sems,
):
    x, y, c, t = place()
    s = lax.axis_index("section")
    loads = {}
    own_load = pltpu.make_async_copy(ends.at[t], x_own, io_sems.at[0])
    own_load.start()
    for n, (start, size) in enumerate(CHUNKS):
        for half in (0, 1):
            part = pl.ds(start, size)
            load = pltpu.make_async_copy(
                full.at[half, :, part], w.at[half, :, part], load_sems.at[2 * n + half]
            )
            load.start()
            loads[n, half] = load

    meet(x, y, c, t)
    send = Sender(send_sems, recv_sems)
    sibling = {"dp": dp_at(x, y, 1 - c)}
    given = {}

    def ready(n):
        for half in (0, 1):
            if (n, half) in loads:
                loads.pop((n, half)).wait()

    length = lengths[t, 0]
    first_half = lax.broadcasted_iota(jnp.int32, (ROWS, 128), 1) < HD
    valid = lax.broadcasted_iota(jnp.int32, (ROWS, ROWS), 1) < length
    scale = HD**-0.5

    def pick(e, value):
        return jnp.where(first_half == (e == 0), value, jnp.zeros_like(value))

    def forward(x):
        ready(0)

        def project(i):
            half, j = lax.div(i, 3), lax.rem(i, 3)
            p = dot(x[...], w[half, :, columns(j * BLOCK, BLOCK)])
            at = columns(half * BLOCK, BLOCK)

            @pl.when(j == 0)
            def _():
                q[:, at] = low(p + b_qv[0:1, at])

            @pl.when(j == 1)
            def _():
                k[:, at] = low(p)

            @pl.when(j == 2)
            def _():
                v[:, at] = low(p + b_qv[1:2, at])

        each(6, project)

        def heads(i):
            at = columns(i * 128, 128)
            kp, vp, qp = k[:, at], v[:, at], q[:, at]
            outs = []
            for e in (0, 1):
                scores = dot_nt(pick(e, qp), kp) * scale
                scores = jnp.where(valid, scores, -1e9)
                powers = jnp.exp(scores - jnp.max(scores, -1, keepdims=True))
                p = powers / jnp.sum(powers, -1, keepdims=True)
                probs[2 * i + e] = p
                outs.append(dot(low(p), vp))
            o[:, at] = low(jnp.where(first_half, outs[0], outs[1]))

        each(8, heads)
        ready(1)
        attended = dot_nt(o[:, 0:512], w[0, :, 1536:2048]) + dot_nt(o[:, 512:1024], w[1, :, 1536:2048])
        normed, inverse = normalize(high(x[...]) + attended + shifts[0:1])
        n1[...], i1[...] = normed, inverse
        hidden = normed * gains[0:1] + shifts[1:2]
        res[...] = hidden
        hid[...] = low(hidden)
        ready(2)

        def widen(i):
            half, j = lax.div(i, 4), lax.rem(i, 4)
            at = columns(i * BLOCK, BLOCK)
            u = dot(hid[...], w[half, :, columns(UP + j * BLOCK, BLOCK)]) + b_ff[:, at]
            phi = 0.5 + 0.5 * lax.erf(u * 0.7071067811865476)
            act[:, at] = low(u * phi)
            slope[:, at] = low(phi + u * (jnp.exp(u * u * -0.5) * 0.3989422804014327))

        each(8, widen)
        ready(3)

        def narrow(i):
            at = columns(i * 256, 256)
            rows = pl.ds(pl.multiple_of(i * 256, 256), 256)
            acc[:, at] = dot_nt(act[:, 0:2048], w[0, rows, DOWN:COLS]) + dot_nt(
                act[:, 2048:4096], w[1, rows, DOWN:COLS]
            )

        each(4, narrow)
        normed, inverse = normalize(res[...] + acc[...] + shifts[2:3])
        n2[...], i2[...] = normed, inverse
        return low(normed * gains[1:2] + shifts[3:4])

    def backward(grad_out, after=lambda stage: None):
        normed = n2[...]
        d_gains[1:2] = total(grad_out * normed)
        d_shifts[3:4] = total(grad_out)
        d_sum = norm_backward(grad_out * gains[1:2], normed, i2[...])
        d_shifts[2:3] = total(d_sum)
        res[...] = d_sum
        d_low[...] = low(d_sum)
        after("d_low")

        def widen(i):
            half, j = lax.div(i, 4), lax.rem(i, 4)
            at = columns(i * BLOCK, BLOCK)
            d = low(dot(d_low[...], w[half, :, columns(DOWN + j * BLOCK, BLOCK)]) * high(slope[:, at]))
            d_act[:, at] = d
            d_bff[:, at] = total(high(d))

        each(8, widen)
        after("d_act")

        def narrow(i):
            at = columns(i * 256, 256)
            rows = pl.ds(pl.multiple_of(i * 256, 256), 256)
            acc[:, at] = dot_nt(d_act[:, 0:2048], w[0, rows, UP:DOWN]) + dot_nt(
                d_act[:, 2048:4096], w[1, rows, UP:DOWN]
            )

        each(4, narrow)
        d_hidden = res[...] + acc[...]
        normed = n1[...]
        d_gains[0:1] = total(d_hidden * normed)
        d_shifts[1:2] = total(d_hidden)
        d_sum = norm_backward(d_hidden * gains[0:1], normed, i1[...])
        d_shifts[0:1] = total(d_sum)
        res[...] = d_sum
        a_low[...] = low(d_sum)
        after("a_low")

        def heads(i):
            at = columns(i * 128, 128)
            half = lax.div(i, 4)
            d_o = low(dot(a_low[...], w[half, :, columns(1536 + lax.rem(i, 4) * 128, 128)]))
            kp, vp, qp = k[:, at], v[:, at], q[:, at]
            parts = []
            for e in (0, 1):
                p = probs[2 * i + e]
                d_p = dot_nt(pick(e, d_o), vp)
                d_s = low(p * (d_p - jnp.sum(p * d_p, -1, keepdims=True)))
                parts.append((dot(d_s, kp) * scale, dot_tn(d_s, qp) * scale, dot_tn(low(p), d_o)))
            d_q, d_k, d_v = (low(jnp.where(first_half, a, b)) for a, b in zip(*parts))
            d_qkv[0, :, at] = d_q
            d_qkv[1, :, at] = d_k
            d_qkv[2, :, at] = d_v
            d_bqv[0:1, at] = total(high(d_q))
            d_bqv[1:2, at] = total(high(d_v))

        each(8, heads)
        after("d_qkv")

        def narrow_in(i):
            at = columns(i * 256, 256)
            rows = pl.ds(pl.multiple_of(i * 256, 256), 256)
            acc[:, at] = sum(
                dot_nt(d_qkv[j, :, 512 * half : 512 * half + 512], w[half, rows, 512 * j : 512 * j + 512])
                for half in (0, 1)
                for j in (0, 1, 2)
            )

        each(4, narrow_in)
        return low(res[...] + acc[...])

    other_half = columns((1 - c) * 2048, 2048)
    other_heads = columns((1 - c) * 512, 512)

    def swap(name, src, dst):
        given[name] = send(src, dst, sibling)

    def have(*names):
        for name in names:
            given[name].wait_recv()

    def block(start, left, right, s_left, s_right):
        whole = low(dot_tn(left, right) + dot_tn(s_left, s_right))
        for chip in range(16):
            for h in (0, 1):
                f, g = (chip // 4, chip % 4) if h == 0 else (chip % 4, chip // 4)
                to, of = h * 512 + f * 128 + g * 32, chip * 64 + h * 32
                w[0, to : to + 32, columns(start, right.shape[1])] = whole[of : of + 32]

    def grads_down():
        have("act", "d_low")

        def one(i):
            at = columns(i * BLOCK, BLOCK)
            block(DOWN + i * BLOCK, d_low[...], act[:, columns(c * 2048 + i * BLOCK, BLOCK)], s_d_low[...], s_act[:, at])

        each(4, one)

    def grads_up():
        have("hid", "d_act")

        def one(i):
            at = columns(i * BLOCK, BLOCK)
            block(UP + i * BLOCK, hid[...], d_act[:, columns(c * 2048 + i * BLOCK, BLOCK)], s_hid[...], s_d_act[:, at])

        each(4, one)

    def spread(row, size, offset):
        lanes = row.shape[1]
        wide = (32, lanes)
        owner = lax.broadcasted_iota(jnp.int32, wide, 0) == lax.div(
            lax.broadcasted_iota(jnp.int32, wide, 1), size
        )
        fold = lax.rem(lax.broadcasted_iota(jnp.int32, (lanes, 128), 0), size) == lax.broadcasted_iota(
            jnp.int32, (lanes, 128), 1
        )
        table = dot(low(jnp.where(owner, row, 0.0)), low(jnp.where(fold, 1.0, 0.0)))
        back = (128, 1024)
        lane = lax.broadcasted_iota(jnp.int32, back, 1)
        source = lax.broadcasted_iota(jnp.int32, back, 0)
        span = min(size, 32)
        place_in = lax.rem(lane, 32)
        if size == 16:
            open_ = (place_in == source + offset) & (source < span)
        else:
            open_ = (place_in + offset == source) & (source < size)
        rows = dot(low(table), low(jnp.where(open_, 1.0, 0.0)))
        mine = lax.broadcasted_iota(jnp.int32, (32, 1024), 0) == lax.div(
            lax.broadcasted_iota(jnp.int32, (32, 1024), 1), 32
        )
        return total(jnp.where(mine, rows, 0.0))

    def small_rows(half, dst):
        heads_at, units_at = columns(half * 512, 512), columns(half * 2048, 2048)
        dst[...] = jnp.zeros_like(dst)
        dst[0:2] = d_gains[...]
        dst[2:6] = d_shifts[...]
        dst[6:7] = spread(d_bqv[0:1, heads_at], 16, 0) + spread(d_bqv[1:2, heads_at], 16, 16)
        dst[7:8] = spread(d_bff[:, units_at], 64, 0)
        dst[8:9] = spread(d_bff[:, units_at], 64, 32)

    def grads_rest():
        have("o", "a_low", "x", "d_qkv", "small")
        block(1536, a_low[...], o[:, columns(c * 512, 512)], s_a_low[...], s_o[...])
        for j in (0, 1, 2):
            block(j * 512, x_in[...], d_qkv[j, :, columns(c * 512, 512)], s_x[...], s_d_qkv[j])
        summed = small[0] + s_small[...]
        column = low(jnp.concatenate([summed, jnp.zeros((112, 1024), jnp.float32)], axis=0).T)
        for chip in range(16):
            for h in (0, 1):
                f, g = (chip // 4, chip % 4) if h == 0 else (chip % 4, chip // 4)
                to, of = h * 512 + f * 128 + g * 32, chip * 64 + h * 32
                w[0, to : to + 32, EXTRA:UP] = column[of : of + 32]

    sent = {}

    def side(h, phase):
        return x if (h == 0) == (phase == 1) else y

    def rows_at(h, step):
        return pl.ds(pl.multiple_of(h * 512 + lax.rem(side(h, 1) + step, 4) * 128, 128), 128)

    def line_at(h, step):
        start = h * 512 + side(h, 1) * 128 + lax.rem(side(h, 2) + step, 4) * 32
        return pl.ds(pl.multiple_of(start, 32), 32)

    def parts(n):
        start, size, half = PASSES[n]
        return pl.ds(start, size), pl.ds(start, half), pl.ds(start + half, size - half)

    def add(dst, *others):
        def one(i):
            at = pl.ds(pl.multiple_of(i * 16, 16), 16)
            dst[at] = low(sum((high(o[at]) for o in others), high(dst[at])))

        each(dst.shape[0] // 16, one)

    def far(n):
        whole, part_a, part_b = parts(n)
        for h in (0, 1):
            rows = rows_at(h, 2)
            sent[n, h, "far"] = (
                send(w.at[0, rows, part_a], passing.at[h, :, part_a], beside(h, 1, 1, x, y, c)),
                send(w.at[0, rows, part_b], passing.at[h, :, part_b], beside(h, 1, 3, x, y, c)),
            )

    def near(n):
        whole, part_a, part_b = parts(n)
        for h in (0, 1):
            up, down = sent[n, h, "far"]
            up.wait_recv()
            add(w.at[0, rows_at(h, 1), part_a], passing.at[h, :, part_a])
            one = send(w.at[0, rows_at(h, 1), whole], near_p.at[h, :, whole], beside(h, 1, 1, x, y, c))
            down.wait_recv()
            add(w.at[0, rows_at(h, 3), part_b], passing.at[h, :, part_b])
            two = send(w.at[0, rows_at(h, 3), whole], near_m.at[h, :, whole], beside(h, 1, 3, x, y, c))
            sent[n, h, "near"] = (one, two)

    def q_far(n):
        whole, part_a, part_b = parts(n)
        for h in (0, 1):
            for copy in sent[n, h, "near"]:
                copy.wait_recv()
            add(w.at[0, rows_at(h, 0), whole], near_p.at[h, :, whole], near_m.at[h, :, whole])
            rows = line_at(h, 2)
            sent[n, h, "q_far"] = (
                send(w.at[0, rows, part_a], q_passing.at[h, :, part_a], beside(h, 2, 1, x, y, c)),
                send(w.at[0, rows, part_b], q_passing.at[h, :, part_b], beside(h, 2, 3, x, y, c)),
            )

    def q_near(n):
        whole, part_a, part_b = parts(n)
        for h in (0, 1):
            up, down = sent[n, h, "q_far"]
            up.wait_recv()
            add(w.at[0, line_at(h, 1), part_a], q_passing.at[h, :, part_a])
            one = send(w.at[0, line_at(h, 1), whole], q_p.at[h, :, whole], beside(h, 2, 1, x, y, c))
            down.wait_recv()
            add(w.at[0, line_at(h, 3), part_b], q_passing.at[h, :, part_b])
            two = send(w.at[0, line_at(h, 3), whole], q_m.at[h, :, whole], beside(h, 2, 3, x, y, c))
            sent[n, h, "q_near"] = (one, two)

    crossing, handing = {}, {}
    owner, sender = c == t, c != t

    def remote(i, src, dst, where):
        return pltpu.make_async_remote_copy(
            src_ref=src,
            dst_ref=dst,
            send_sem=send_sems.at[N_EACH + i],
            recv_sem=recv_sems.at[N_EACH + i],
            device_id=where,
            device_id_type=MESH,
        )

    def cross(n):
        whole, _, _ = parts(n)
        for h in (0, 1):
            for copy in sent[n, h, "q_near"]:
                copy.wait_recv()
            add(w.at[0, line_at(h, 0), whole], q_p.at[h, :, whole], q_m.at[h, :, whole])
            crossing[n, h] = remote(
                2 * n + h, w.at[0, line_at(h, 0), whole], mate.at[h, :, whole], {"tensor": 1 - t}
            )

            @pl.when(sender)
            def _():
                crossing[n, h].start()

    def hand(n):
        whole, _, _ = parts(n)
        handing[n] = remote(6 + n, to_mate.at[:, whole], out.at[:, whole], sibling)

        @pl.when(owner)
        def _():
            for h in (0, 1):
                crossing[n, h].wait_recv()
                value = high(w[0, line_at(h, 0), whole]) + high(mate[h, :, whole])

                @pl.when(c == h)
                def _():
                    out[:, whole] = value

                @pl.when(c != h)
                def _():
                    to_mate[:, whole] = value

            handing[n].start()

    def exchange(n):
        copy = send(kept.at[n], relay.at[n], {"section": 1 - s})
        copy.wait_recv()
        return relay[n]

    def last_stage(stage):
        if stage == "d_low":
            swap("d_low", d_low, s_d_low)
        if stage == "d_act":
            swap("d_act", d_act.at[:, other_half], s_d_act)
            grads_down()
            far(0)
        if stage == "a_low":
            swap("a_low", a_low, s_a_low)
            grads_up()
            far(1)
            near(0)
        if stage == "d_qkv":
            swap("d_qkv", d_qkv.at[:, :, other_heads], s_d_qkv)
            small_rows(1 - c, small.at[1])
            swap("small", small.at[1], s_small)
            near(1)

    own_load.wait()
    kept[0] = forward(x_own)
    x_in[...] = jnp.where(s == 0, x_own[...], exchange(0))
    swap("x", x_in, s_x)
    result = forward(x_in)
    swap("hid", hid, s_hid)
    swap("act", act.at[:, other_half], s_act)
    swap("o", o.at[:, other_heads], s_o)
    kept[2] = result
    kept[1] = backward(high(x_own[...]))
    grad_out = jnp.where(s == 1, x_own[...], exchange(1))
    d_x = backward(high(grad_out), last_stage)
    kept[2] = jnp.where(s == 0, d_x, kept[2])
    across = send(kept.at[2], ends_out.at[t], {"tensor": 1 - t})
    here = pltpu.make_async_copy(kept.at[2], ends_out.at[t], io_sems.at[1])
    here.start()
    small_rows(c, small.at[0])
    grads_rest()
    far(2)
    q_far(0)
    near(2)
    q_far(1)
    q_near(0)
    q_near(1)
    cross(0)
    q_far(2)
    cross(1)
    hand(0)
    q_near(2)
    hand(1)
    cross(2)
    hand(2)
    for n in (0, 1, 2):

        @pl.when(sender)
        def _():
            handing[n].wait_recv()
            for h in (0, 1):
                crossing[n, h].wait_send()

        @pl.when(owner)
        def _():
            handing[n].wait_send()

    here.wait()
    across.wait_recv()
    send.finish()


def run_layers(lengths, ends, full, gains, shifts, b_qv, b_ff):
    vmem = pltpu.VMEM
    bf, f32 = jnp.bfloat16, jnp.float32
    hbm = pl.BlockSpec(memory_space=pl.ANY)
    near = pl.BlockSpec(memory_space=vmem)
    sem = pltpu.SemaphoreType.DMA
    shape = jax.ShapeDtypeStruct
    return pl.pallas_call(
        layers_kernel,
        out_shape=(
            shape((2, ROWS, 1024), bf),
            shape((32, COLS), f32),
        ),
        in_specs=[pl.BlockSpec(memory_space=pltpu.SMEM), hbm, hbm, near, near, near, near],
        out_specs=(hbm, near),
        scratch_shapes=[
            vmem((2, 1024), f32),
            vmem((4, 1024), f32),
            vmem((2, 1024), f32),
            vmem((1, 4096), f32),
            vmem((2, 1024, COLS), bf),
            vmem((ROWS, 1024), bf),
            vmem((ROWS, 1024), bf),
            vmem((2, ROWS, 1024), bf),
            vmem((ROWS, 1024), bf),
            vmem((ROWS, 1024), bf),
            vmem((ROWS, 1024), bf),
            vmem((ROWS, 1024), bf),
            vmem((16, ROWS, ROWS), f32),
            vmem((ROWS, 1024), f32),
            vmem((ROWS, 1024), f32),
            vmem((ROWS, 1), f32),
            vmem((ROWS, 1), f32),
            vmem((ROWS, 1024), f32),
            vmem((ROWS, 1024), bf),
            vmem((ROWS, 4096), bf),
            vmem((ROWS, 4096), bf),
            vmem((ROWS, 4096), bf),
            vmem((3, ROWS, 1024), bf),
            vmem((ROWS, 1024), f32),
            vmem((ROWS, 1024), bf),
            vmem((ROWS, 1024), bf),
            vmem((3, ROWS, 1024), bf),
            vmem((2, 16, 1024), f32),
            vmem((ROWS, 1024), bf),
            vmem((ROWS, 1024), bf),
            vmem((ROWS, 1024), bf),
            vmem((ROWS, 1024), bf),
            vmem((ROWS, 2048), bf),
            vmem((ROWS, 2048), bf),
            vmem((ROWS, 512), bf),
            vmem((3, ROWS, 512), bf),
            vmem((16, 1024), f32),
            vmem((2, 128, COLS), bf),
            vmem((2, 128, COLS), bf),
            vmem((2, 128, COLS), bf),
            vmem((2, 32, COLS), bf),
            vmem((2, 32, COLS), bf),
            vmem((2, 32, COLS), bf),
            vmem((2, 32, COLS), bf),
            vmem((32, COLS), f32),
            sem((8,)),
            sem((2,)),
            sem((N_EACH + 9,)),
            sem((N_EACH + 9,)),
        ],
        compiler_params=pltpu.CompilerParams(
            collective_id=2, has_side_effects=True, vmem_limit_bytes=62 * 2**20
        ),
        name="run_layers",
    )(lengths, ends, full, gains, shifts, b_qv, b_ff)


def pack_shard(w_qkv, w_out, w_up, w_down, gains, shifts, b_qv, b_ff):
    extra = jnp.concatenate(
        [gains[0].T, shifts[0].T, b_qv[0, :, 0].reshape(32, 1), b_ff[0, 0].reshape(2, 32).T], axis=1
    )
    return jnp.concatenate(
        [
            w_qkv[0].reshape(32, 1536),
            w_out[0].T,
            jnp.pad(extra, ((0, 0), (0, 119))),
            w_up[0],
            w_down[0].T,
        ],
        axis=1,
    )


def unpack_extra(extra):
    extra = extra.astype(jnp.float32)
    gains = extra[0, :, 0:2].T
    shifts = extra[0, :, 2:6].T
    b_qv = extra[:, :, 6].reshape(2, 32, 2, 16).transpose(2, 0, 1, 3).reshape(2, 1024)
    b_ff = extra[:, :, 7:9].reshape(2, 32, 32, 2).transpose(0, 1, 3, 2).reshape(4096)
    return gains, shifts, b_qv, b_ff


def unpack_shard(got):
    extra = got[:, EXTRA:UP]
    return (
        got[:, :1536].reshape(1, 32, 3, 512),
        got[:, 1536:2048].T[None],
        got[:, UP:DOWN][None],
        got[:, DOWN:].T[None],
        extra[:, 0:2].T[None],
        extra[:, 2:6].T[None],
        extra[:, 6].reshape(1, 2, 1, 16),
        extra[:, 7:9].T.reshape(1, 1, 64),
    )


def body(ends, lengths, w_qkv, w_out, w_up, w_down, gains, shifts, b_qv, b_ff):
    full = gather_weights(pack_shard(w_qkv, w_out, w_up, w_down, gains, shifts, b_qv, b_ff))
    gains, shifts, b_qv, b_ff = unpack_extra(full[:, :, EXTRA:UP])
    ends_out, got = run_layers(
        lengths, ends.reshape(2, ROWS, 1024), full, gains, shifts, b_qv, b_ff.reshape(1, 4096)
    )
    return (ends_out.reshape(1, 2, 1, ROWS, 1024),) + unpack_shard(got)


def solution(mesh):
    in_specs = (
        P("section", None, "dp", None, None),
        P(None, "dp"),
        P("section", "dp", None, "tensor"),
        P("section", "tensor", "dp"),
        P("section", "dp", "tensor"),
        P("section", "tensor", "dp"),
        P("section", None, "dp"),
        P("section", None, "dp"),
        P("section", None, "tensor", "dp"),
        P("section", "tensor", "dp"),
    )
    out_specs = (
        P("section", None, "dp", None, None),
        P("section", "dp", None, "tensor"),
        P("section", "tensor", "dp"),
        P("section", "dp", "tensor"),
        P("section", "tensor", "dp"),
        P("section", None, "dp"),
        P("section", None, "dp"),
        P("section", None, "tensor", "dp"),
        P("section", "tensor", "dp"),
    )
    return jax.shard_map(body, mesh=mesh, in_specs=in_specs, out_specs=out_specs, check_vma=False)
```

time: 304 us -> 280 us (0.921)
  Pallas kernels: 277 us -> 252 us
  local copies, waits for them, and re-layouts: 19 us -> 23.9 us
    pallas_call x1 -> x0, Pallas kernels: 78.7 us -> none  [scatter_grads(): pl.pallas_call(scatter_kernel, out_shape=jax.ShapeDtypeStruct((2, 16, col...]
    pallas_call x1, Pallas kernels: 116 us -> 174 us  [run_layers(): pl.pallas_call(layers_kernel, out_shape=(shape((2, ROWS, 1024), bf), shap...]
    pallas_call x1, Pallas kernels: 82 us -> 78.7 us  [gather_weights(): pl.pallas_call(gather_kernel, out_shape=jax.ShapeDtypeStruct((2, 4, 4, 2,...]
    unnamed x17 -> x13, local copies, waits for them, and re-layouts: 7.43 us -> 8.34 us
where the time goes in v1:
time: 280 us; the launch traced here: 279 us
  Pallas kernels  252 us (90%)
  local copies, waits for them, and re-layouts  23.9 us (9%)
    pallas_call x1, Pallas kernels, run_layers(): pl.pallas_call(layers_kernel, out_shape=(shape((2, ROWS, 1024), bf), shap...  174 us
    pallas_call x1, Pallas kernels, gather_weights(): pl.pallas_call(gather_kernel, out_shape=jax.ShapeDtypeStruct((2, 4, 4, 2,...  78.7 us
    unnamed x13, local copies, waits for them, and re-layouts  8.34 us

profile of v1, /device:TPU:1, one launch (start us, length us, event | category | flops | bytes accessed | tf_op | source)
XLA Modules:
  0.0 279.0 jit_solution(2570976228150524130)
XLA Ops:
  0.6 0.5 broadcast.7
  1.2 1.3 reduce.7
  2.5 0.1 reshape_squeeze.14
  2.6 0.7 reshape_squeeze.13
  3.3 1.3 copy.37.lengths
  4.6 0.7 pad_maximum_fusion
  5.3 0.1 copy.45
  5.4 1.0 copy.32
  6.4 0.1 concatenate.17
  6.5 0.8 constant_dynamic-update-slice_fusion.3
  7.3 0.9 constant_dynamic-update-slice_fusion.1
  8.2 0.9 constant_dynamic-update-slice_fusion.shard
  9.2 0.0 copy-start
  9.2 0.7 copy-done
  9.9 78.7 %gather_weights.1 = bf16[2,4,4,2,2,16,6272]{6,5,4,3,2,1,0:T(8,128)(2,1)} custom-call(bf16[2,16,6272]{2,1,0:T(8,128)(2,1)} %copy-done), custom_call_target="tpu_custom_call" | custom-call | tf_op jit(solution)/shard_map/gather_weights/pallas_call | solution.py:179
  88.7 1.1 slice.57
  89.7 0.2 copy.44
  90.0 0.1 reshape.50
  90.1 0.1 copy.47
  90.1 0.7 reshape_reshape.3.b_ff
  90.9 0.1 convert_element_type.5
  91.0 0.6 slice_bitcast_fusion.7.gains
  91.6 0.6 slice_bitcast_fusion.3.shifts
  92.2 0.1 reshape_squeeze.15
  92.4 0.7 reshape.49.b_qv
  93.1 173.5 %run_layers.1 = (bf16[2,192,1024]{2,1,0:T(8,128)(2,1)}, f32[32,6272]{1,0:T(8,128)}) custom-call(s32[2,1]{1,0:T(2,128)} %copy.37.lengths, bf16[2,192,1024]{2,1,0:T(8,128)(2,1)} %bitcast.63, bf16[2,1024,6272]{2,1,0:T(8,128)(2,1)} %bitcast.62, f32[2,1024]{1,0:T(2,128)} %slice_bitcast_fusion.7.gains, f32[4,1024]{1,0:T(4,128)} %slice_bitcast_fusion.3.shifts, ...), custom_call_target="tpu_custom_call" | custom-call | tf_op jit(solution)/shard_map/run_layers/pallas_call | solution.py:702
  266.6 0.9 slice_reduce_fusion
  267.5 0.7 reshape_squeeze.16
  268.1 0.8 slice_bitcast_fusion.5
  268.9 0.7 copy.39
  269.6 0.9 slice_bitcast_fusion.4
  270.4 0.1 copy.40
  270.5 0.6 reshape.53
  271.1 0.6 copy.38
  271.8 1.5 slice_bitcast_fusion.2
  273.2 0.9 slice.49
  274.2 1.9 slice_bitcast_fusion
  276.0 0.1 reshape.52
  276.2 0.7 copy.42
  276.9 2.1 copy.53
  (6 shorter events, 0.1 us)
Async XLA Ops:
  9.2 0.8 copy-start

commit v2 on v1

--- a/solution.py
+++ b/solution.py
@@ -12,11 +12,10 @@
 ROWS = 192
 BLOCK = 512
 EXTRA, UP, DOWN = 2048, 2176, 4224
-CHUNKS = ((0, 1536), (1536, 512), (UP, 2048), (DOWN, 2048))
+GATHERS = ((0, 2176, 1152), (UP, 2048, 1024), (DOWN, 2048, 1024))
 PASSES = ((DOWN, 2048, 1024), (UP, 2048, 1024), (0, 2176, 1152))
 
 
-HALF_A = 3200
 OFFSETS = (0, 3, 1, 2)
 MESH = pl.DeviceIdType.MESH
 
@@ -75,124 +74,8 @@
             copy.wait_send()
 
 
-N_GATHER = 143
-
-
-def gather_kernel(shard, out, local_sem, send_sems, recv_sems):
-    x, y, c, t = place()
-    cols = shard.shape[-1]
-    part_a, part_b = pl.ds(0, HALF_A), pl.ds(HALF_A, cols - HALF_A)
-    meet(x, y, c, t)
-    send = Sender(send_sems, recv_sems)
-    sibling = {"dp": dp_at(x, y, 1 - c)}
-    own = out.at[t, x, y, c]
-    local = pltpu.make_async_copy(shard, own, local_sem)
-    local.start()
-    from_partner = send(shard, own, {"tensor": 1 - t})
-    to_sibling = [send(shard, own, sibling)]
-
-    def block(k, h, ja, jb):
-        a, b = OFFSETS[ja], OFFSETS[jb]
-        dx, dy = (a, b) if h == 0 else (b, a)
-        return out.at[t if k == 0 else 1 - t, lax.rem(x + dx, 4), lax.rem(y + dy, 4), c, h]
-
-    def both(k, h, phase, ja):
-        dst = block(k, h, ja, 0)
-        src = shard.at[h] if (k == 0 and ja == 0) else dst
-        return (
-            send(src, dst, beside(h, phase, 1, x, y, c)),
-            send(src, dst, beside(h, phase, 3, x, y, c)),
-        )
-
-    def take(k, h, phase, ja, pair):
-        onward = []
-        for copy, j, part, step in ((pair[0], 1, part_a, 1), (pair[1], 2, part_b, 3)):
-            copy.wait_recv()
-            here = block(k, h, *((j, 0) if phase == 1 else (ja, j)))
-            onward.append(send(here.at[:, part], here.at[:, part], beside(h, phase, step, x, y, c)))
-            to_sibling.append(send(here, here, sibling))
-        return onward
-
-    first, second = {}, {}
-
-    def begin(k):
-        for h in (0, 1):
-            first[k, h] = both(k, h, 1, 0)
-        for h in (0, 1):
-            second[k, h, 0] = both(k, h, 2, 0)
-
-    mate = out.at[1 - t, x, y, c]
-    onward, last = {}, {}
-
-    def first_in(k):
-        for h in (0, 1):
-            onward[k, h] = take(k, h, 1, 0, first[k, h])
-        for h in (0, 1):
-            for ja in (1, 2):
-                second[k, h, ja] = both(k, h, 2, ja)
-
-    def far_in(k):
-        for h in (0, 1):
-            for copy in onward[k, h]:
-                copy.wait_recv()
-            second[k, h, 3] = both(k, h, 2, 3)
-            here = block(k, h, 3, 0)
-            to_sibling.append(send(here, here, sibling))
-
-    def second_in(k, *places):
-        for ja in places:
-            for h in (0, 1):
-                last[k, h, ja] = take(k, h, 2, ja, second[k, h, ja])
-
-    def last_in(k):
-        for ja in (0, 1, 2, 3):
-            for h in (0, 1):
-                for copy in last[k, h, ja]:
-                    copy.wait_recv()
-                here = block(k, h, ja, 3)
-                to_sibling.append(send(here, here, sibling))
-
-    begin(0)
-    first_in(0)
-    from_partner.wait_recv()
-    begin(1)
-    to_sibling.append(send(mate, mate, sibling))
-    far_in(0)
-    second_in(0, 0)
-    first_in(1)
-    second_in(0, 1, 2)
-    far_in(1)
-    second_in(1, 0)
-    second_in(0, 3)
-    second_in(1, 1, 2)
-    last_in(0)
-    second_in(1, 3)
-    last_in(1)
-    local.wait()
-    for copy in to_sibling:
-        copy.wait_recv()
-    send.finish()
-
-
-def gather_weights(shard):
-    rows, cols = shard.shape
-    out = pl.pallas_call(
-        gather_kernel,
-        out_shape=jax.ShapeDtypeStruct((2, 4, 4, 2, 2, 16, cols), jnp.bfloat16),
-        in_specs=[pl.BlockSpec(memory_space=pl.ANY)],
-        out_specs=pl.BlockSpec(memory_space=pl.ANY),
-        scratch_shapes=[
-            pltpu.SemaphoreType.DMA,
-            pltpu.SemaphoreType.DMA((N_GATHER,)),
-            pltpu.SemaphoreType.DMA((N_GATHER,)),
-        ],
-        compiler_params=pltpu.CompilerParams(collective_id=0, has_side_effects=True),
-        name="gather_weights",
-    )(shard.reshape(2, 16, cols))
-    return out.reshape(2, 32 * rows, cols)
-
-
 N_EACH = 60
+N_GATHER = 147
 
 
 def dot(a, b):
@@ -242,38 +125,130 @@
 
 
 def layers_kernel(
-    lengths, ends, full, gains, shifts, b_qv, b_ff,
+    lengths, ends, my_qkv, my_out, my_up, my_down, my_small,
     ends_out, out,
+    gains, shifts, b_qv, b_ff,
     d_gains, d_shifts, d_bqv, d_bff,
-    w, x_own, x_in, relay, q, k, v, o, probs, n1, n2, i1, i2, res, hid, act, slope, d_act, d_qkv,
+    blocks, x_own, x_in, relay, q, k, v, o, probs, n1, n2, i1, i2, res, hid, act, slope, d_act, d_qkv,
     acc, d_low, a_low, kept, small,
     s_x, s_hid, s_d_low, s_a_low, s_act, s_d_act, s_o, s_d_qkv, s_small,
     passing, near_p, near_m, q_passing, q_p, q_m, mate, to_mate,
-    load_sems, io_sems, send_sems, recv_sems,
+    io_sems, send_sems, recv_sems, gather_send_sems, gather_recv_sems,
 ):
     x, y, c, t = place()
     s = lax.axis_index("section")
-    loads = {}
+    w = blocks.reshape(2, 1024, COLS)
     own_load = pltpu.make_async_copy(ends.at[t], x_own, io_sems.at[0])
     own_load.start()
-    for n, (start, size) in enumerate(CHUNKS):
-        for half in (0, 1):
-            part = pl.ds(start, size)
-            load = pltpu.make_async_copy(
-                full.at[half, :, part], w.at[half, :, part], load_sems.at[2 * n + half]
-            )
-            load.start()
-            loads[n, half] = load
-
+    own = blocks.at[t, x, y, c]
+    own[:, :, 0:1536] = my_qkv[...].reshape(2, 16, 1536)
+    own[:, :, 1536:EXTRA] = my_out[...].reshape(2, 16, 512)
+    own[:, :, EXTRA:UP] = low(my_small[...].T)[0:32].reshape(2, 16, 128)
+    own[:, :, UP:DOWN] = my_up[...].reshape(2, 16, 2048)
+    own[:, :, DOWN:COLS] = my_down[...].reshape(2, 16, 2048)
     meet(x, y, c, t)
     send = Sender(send_sems, recv_sems)
+    share = Sender(gather_send_sems, gather_recv_sems)
     sibling = {"dp": dp_at(x, y, 1 - c)}
-    given = {}
-
-    def ready(n):
+    given, shared, to_sibling = {}, {}, {0: [], 1: [], 2: []}
+
+    def half_block(n, kk, h, step):
+        start, size, _ = GATHERS[n]
+        tt = t if kk == 0 else 1 - t
+        xx, yy = (lax.rem(x + step, 4), y) if h == 0 else (x, lax.rem(y + step, 4))
+        return blocks.at[tt, xx, yy, c, h, :, pl.ds(start, size)]
+
+    def lane_of(n, kk, h, step):
+        start, size, _ = GATHERS[n]
+        tt = t if kk == 0 else 1 - t
+        if h == 0:
+            return blocks.at[tt, :, lax.rem(y + step, 4), c, 0, :, pl.ds(start, size)]
+        return blocks.at[tt, lax.rem(x + step, 4), :, c, 1, :, pl.ds(start, size)]
+
+    def part_of(n, ref, first):
+        _, size, half = GATHERS[n]
+        part = pl.ds(0, half) if first else pl.ds(half, size - half)
+        return ref.at[:, part] if len(ref.shape) == 2 else ref.at[:, :, part]
+
+    def first_send(n, kk):
+        for h in (0, 1):
+            src = half_block(n, kk, h, 0)
+            shared[n, kk, h, 1] = [share(src, src, beside(h, 1, step, x, y, c)) for step in (1, 3)]
+
+    def pass_on(n, kk, h, phase, find):
+        onward = []
+        for copy, step in zip(shared[n, kk, h, phase], (1, 3)):
+            copy.wait_recv()
+            here = find(n, kk, h, 4 - step)
+            part = part_of(n, here, step == 1)
+            onward.append(share(part, part, beside(h, phase, step, x, y, c)))
+            if phase == 2:
+                to_sibling[n].append(share(here, here, sibling))
+        shared[n, kk, h, phase] = onward
+
+    def first_on(n, kk):
+        for h in (0, 1):
+            pass_on(n, kk, h, 1, half_block)
+
+    def second_send(n, kk):
+        for h in (0, 1):
+            for copy in shared[n, kk, h, 1]:
+                copy.wait_recv()
+            src = lane_of(n, kk, h, 0)
+            shared[n, kk, h, 2] = [share(src, src, beside(h, 2, step, x, y, c)) for step in (1, 3)]
+            to_sibling[n].append(share(src, src, sibling))
+
+    def second_on(n, kk):
+        for h in (0, 1):
+            pass_on(n, kk, h, 2, lane_of)
+
+    def second_end(n, kk):
+        for h in (0, 1):
+            for copy in shared[n, kk, h, 2]:
+                copy.wait_recv()
+            here = lane_of(n, kk, h, 2)
+            to_sibling[n].append(share(here, here, sibling))
+
+    def complete(n):
+        for copy in to_sibling[n]:
+            copy.wait_recv()
+
+    def collect(half, rows):
+        wide = (32, 1024)
+        owner_of = lax.broadcasted_iota(jnp.int32, wide, 0) == lax.div(
+            lax.broadcasted_iota(jnp.int32, wide, 1), 32
+        )
+        fold = lax.rem(lax.broadcasted_iota(jnp.int32, (1024, 128), 0), 32) == lax.broadcasted_iota(
+            jnp.int32, (1024, 128), 1
+        )
+        fold = low(jnp.where(fold, 1.0, 0.0))
+        tables = [low(dot(low(jnp.where(owner_of, row, 0.0)), fold)) for row in rows]
+
+        def open_up(size, *terms):
+            lanes = size * 32
+            lane = lax.broadcasted_iota(jnp.int32, (128, lanes), 1)
+            source = lax.broadcasted_iota(jnp.int32, (128, lanes), 0)
+            found = jnp.zeros((32, lanes), jnp.float32)
+            for table, offset in terms:
+                pick_at = (lax.rem(lane, size) + offset == source) & (source < 32)
+                found = found + dot(table, low(jnp.where(pick_at, 1.0, 0.0)))
+            mine = lax.broadcasted_iota(jnp.int32, (32, lanes), 0) == lax.div(
+                lax.broadcasted_iota(jnp.int32, (32, lanes), 1), size
+            )
+            return total(jnp.where(mine, found, 0.0))
+
+        at = pl.ds(half * 512, 512)
+        b_qv[0:1, at] = open_up(16, (tables[0], 0))
+        b_qv[1:2, at] = open_up(16, (tables[0], 16))
+        b_ff[:, pl.ds(half * 2048, 2048)] = open_up(64, (tables[1], 0), (tables[2], -32))
+
+    def take_parameters():
         for half in (0, 1):
-            if (n, half) in loads:
-                loads.pop((n, half)).wait()
+            rows = high(w[half, :, EXTRA:UP]).T
+            if half == 0:
+                gains[...] = rows[0:2]
+                shifts[...] = rows[2:6]
+            collect(half, (rows[6:7], rows[7:8], rows[8:9]))
 
     length = lengths[t, 0]
     first_half = lax.broadcasted_iota(jnp.int32, (ROWS, 128), 1) < HD
@@ -283,8 +258,7 @@
     def pick(e, value):
         return jnp.where(first_half == (e == 0), value, jnp.zeros_like(value))
 
-    def forward(x):
-        ready(0)
+    def forward(x, after=lambda stage: None):
 
         def project(i):
             half, j = lax.div(i, 3), lax.rem(i, 3)
@@ -304,6 +278,7 @@
                 v[:, at] = low(p + b_qv[1:2, at])
 
         each(6, project)
+        after("qkv")
 
         def heads(i):
             at = columns(i * 128, 128)
@@ -313,20 +288,20 @@
                 scores = dot_nt(pick(e, qp), kp) * scale
                 scores = jnp.where(valid, scores, -1e9)
                 powers = jnp.exp(scores - jnp.max(scores, -1, keepdims=True))
-                p = powers / jnp.sum(powers, -1, keepdims=True)
+                p = low(powers / jnp.sum(powers, -1, keepdims=True))
                 probs[2 * i + e] = p
-                outs.append(dot(low(p), vp))
+                outs.append(dot(p, vp))
             o[:, at] = low(jnp.where(first_half, outs[0], outs[1]))
 
         each(8, heads)
-        ready(1)
+        after("heads")
         attended = dot_nt(o[:, 0:512], w[0, :, 1536:2048]) + dot_nt(o[:, 512:1024], w[1, :, 1536:2048])
         normed, inverse = normalize(high(x[...]) + attended + shifts[0:1])
         n1[...], i1[...] = normed, inverse
         hidden = normed * gains[0:1] + shifts[1:2]
         res[...] = hidden
         hid[...] = low(hidden)
-        ready(2)
+        after("hid")
 
         def widen(i):
             half, j = lax.div(i, 4), lax.rem(i, 4)
@@ -337,7 +312,7 @@
             slope[:, at] = low(phi + u * (jnp.exp(u * u * -0.5) * 0.3989422804014327))
 
         each(8, widen)
-        ready(3)
+        after("act")
 
         def narrow(i):
             at = columns(i * 256, 256)
@@ -396,10 +371,11 @@
             kp, vp, qp = k[:, at], v[:, at], q[:, at]
             parts = []
             for e in (0, 1):
-                p = probs[2 * i + e]
+                p_low = probs[2 * i + e]
+                p = high(p_low)
                 d_p = dot_nt(pick(e, d_o), vp)
                 d_s = low(p * (d_p - jnp.sum(p * d_p, -1, keepdims=True)))
-                parts.append((dot(d_s, kp) * scale, dot_tn(d_s, qp) * scale, dot_tn(low(p), d_o)))
+                parts.append((dot(d_s, kp) * scale, dot_tn(d_s, qp) * scale, dot_tn(p_low, d_o)))
             d_q, d_k, d_v = (low(jnp.where(first_half, a, b)) for a, b in zip(*parts))
             d_qkv[0, :, at] = d_q
             d_qkv[1, :, at] = d_k
@@ -643,8 +619,54 @@
             swap("small", small.at[1], s_small)
             near(1)
 
+    def first_stage(stage):
+        if stage == "qkv":
+            second_on(1, 0)
+            second_send(2, 0)
+            first_on(2, 1)
+        if stage == "heads":
+            second_on(1, 1)
+            second_send(2, 1)
+        if stage == "hid":
+            second_end(1, 0)
+            second_end(1, 1)
+            second_on(2, 0)
+            complete(1)
+        if stage == "act":
+            second_on(2, 1)
+            second_end(2, 0)
+            second_end(2, 1)
+            complete(2)
+
+    z_sends = []
+    for n, (start, size, _) in enumerate(GATHERS):
+        part = own.at[:, :, pl.ds(start, size)]
+        z_sends.append(share(part, part, {"tensor": 1 - t}))
+        first_send(n, 0)
+    first_on(0, 0)
+    z_sends[0].wait_recv()
+    first_send(0, 1)
+    second_send(0, 0)
+    first_on(0, 1)
+    first_on(1, 0)
+    second_send(0, 1)
+    z_sends[1].wait_recv()
+    first_send(1, 1)
+    second_on(0, 0)
+    second_send(1, 0)
+    first_on(1, 1)
+    second_on(0, 1)
+    z_sends[2].wait_recv()
+    first_on(2, 0)
+    first_send(2, 1)
+    second_send(1, 1)
+    second_end(0, 0)
+    second_end(0, 1)
+    complete(0)
+    take_parameters()
     own_load.wait()
-    kept[0] = forward(x_own)
+    kept[0] = forward(x_own, first_stage)
+    share.finish()
     x_in[...] = jnp.where(s == 0, x_own[...], exchange(0))
     swap("x", x_in, s_x)
     result = forward(x_in)
@@ -692,7 +714,7 @@
     send.finish()
 
 
-def run_layers(lengths, ends, full, gains, shifts, b_qv, b_ff):
+def run_layers(lengths, ends, *shards):
     vmem = pltpu.VMEM
     bf, f32 = jnp.bfloat16, jnp.float32
     hbm = pl.BlockSpec(memory_space=pl.ANY)
@@ -705,14 +727,18 @@
             shape((2, ROWS, 1024), bf),
             shape((32, COLS), f32),
         ),
-        in_specs=[pl.BlockSpec(memory_space=pltpu.SMEM), hbm, hbm, near, near, near, near],
+        in_specs=[pl.BlockSpec(memory_space=pltpu.SMEM), hbm, near, near, near, near, near],
         out_specs=(hbm, near),
         scratch_shapes=[
             vmem((2, 1024), f32),
             vmem((4, 1024), f32),
             vmem((2, 1024), f32),
             vmem((1, 4096), f32),
-            vmem((2, 1024, COLS), bf),
+            vmem((2, 1024), f32),
+            vmem((4, 1024), f32),
+            vmem((2, 1024), f32),
+            vmem((1, 4096), f32),
+            vmem((2, 4, 4, 2, 2, 16, COLS), bf),
             vmem((ROWS, 1024), bf),
             vmem((ROWS, 1024), bf),
             vmem((2, ROWS, 1024), bf),
@@ -720,7 +746,7 @@
             vmem((ROWS, 1024), bf),
             vmem((ROWS, 1024), bf),
             vmem((ROWS, 1024), bf),
-            vmem((16, ROWS, ROWS), f32),
+            vmem((16, ROWS, ROWS), bf),
             vmem((ROWS, 1024), f32),
             vmem((ROWS, 1024), f32),
             vmem((ROWS, 1), f32),
@@ -753,41 +779,28 @@
             vmem((2, 32, COLS), bf),
             vmem((2, 32, COLS), bf),
             vmem((32, COLS), f32),
-            sem((8,)),
             sem((2,)),
             sem((N_EACH + 9,)),
             sem((N_EACH + 9,)),
+            sem((N_GATHER,)),
+            sem((N_GATHER,)),
         ],
         compiler_params=pltpu.CompilerParams(
-            collective_id=2, has_side_effects=True, vmem_limit_bytes=62 * 2**20
+            collective_id=0, has_side_effects=True, vmem_limit_bytes=62 * 2**20
         ),
         name="run_layers",
-    )(lengths, ends, full, gains, shifts, b_qv, b_ff)
+    )(lengths, ends, *shards)
 
 
 def pack_shard(w_qkv, w_out, w_up, w_down, gains, shifts, b_qv, b_ff):
-    extra = jnp.concatenate(
-        [gains[0].T, shifts[0].T, b_qv[0, :, 0].reshape(32, 1), b_ff[0, 0].reshape(2, 32).T], axis=1
+    small = jnp.concatenate([gains[0], shifts[0], b_qv.reshape(1, 32), b_ff.reshape(2, 32)], axis=0)
+    return (
+        w_qkv[0].reshape(32, 1536),
+        w_out[0].T,
+        w_up[0],
+        w_down[0].T,
+        jnp.pad(small.astype(jnp.float32), ((0, 119), (0, 96))),
     )
-    return jnp.concatenate(
-        [
-            w_qkv[0].reshape(32, 1536),
-            w_out[0].T,
-            jnp.pad(extra, ((0, 0), (0, 119))),
-            w_up[0],
-            w_down[0].T,
-        ],
-        axis=1,
-    )
-
-
-def unpack_extra(extra):
-    extra = extra.astype(jnp.float32)
-    gains = extra[0, :, 0:2].T
-    shifts = extra[0, :, 2:6].T
-    b_qv = extra[:, :, 6].reshape(2, 32, 2, 16).transpose(2, 0, 1, 3).reshape(2, 1024)
-    b_ff = extra[:, :, 7:9].reshape(2, 32, 32, 2).transpose(0, 1, 3, 2).reshape(4096)
-    return gains, shifts, b_qv, b_ff
 
 
 def unpack_shard(got):
@@ -805,11 +818,8 @@
 
 
 def body(ends, lengths, w_qkv, w_out, w_up, w_down, gains, shifts, b_qv, b_ff):
-    full = gather_weights(pack_shard(w_qkv, w_out, w_up, w_down, gains, shifts, b_qv, b_ff))
-    gains, shifts, b_qv, b_ff = unpack_extra(full[:, :, EXTRA:UP])
-    ends_out, got = run_layers(
-        lengths, ends.reshape(2, ROWS, 1024), full, gains, shifts, b_qv, b_ff.reshape(1, 4096)
-    )
+    shards = pack_shard(w_qkv, w_out, w_up, w_down, gains, shifts, b_qv, b_ff)
+    ends_out, got = run_layers(lengths, ends.reshape(2, ROWS, 1024), *shards)
     return (ends_out.reshape(1, 2, 1, ROWS, 1024),) + unpack_shard(got)
 
 

time: 280 us -> 250 us (0.89)
  Pallas kernels: 252 us -> 232 us
  local copies, waits for them, and re-layouts: 23.9 us -> 15.6 us
    pallas_call x1 -> x0, Pallas kernels: 78.7 us -> none  [gather_weights(): pl.pallas_call(gather_kernel, out_shape=jax.ShapeDtypeStruct((2, 4, 4, 2,...]
    pallas_call x1, Pallas kernels: 174 us -> 232 us  [run_layers(): pl.pallas_call(layers_kernel, out_shape=(shape((2, ROWS, 1024), bf), shap...]
    unnamed x13 -> x18, local copies, waits for them, and re-layouts: 8.34 us -> 5.82 us
where the time goes in v2:
time: 250 us
  Pallas kernels  232 us (93%)
  local copies, waits for them, and re-layouts  15.6 us (6%)
    pallas_call x1, Pallas kernels, run_layers(): pl.pallas_call(layers_kernel, out_shape=(shape((2, ROWS, 1024), bf), shap...  232 us
    unnamed x18, local copies, waits for them, and re-layouts  5.82 us

profile of v2, /device:TPU:1, one launch (start us, length us, event | category | flops | bytes accessed | tf_op | source)
XLA Modules:
  0.0 249.6 jit_solution(16756316701270032838)
XLA Ops:
  0.6 0.0 copy-start.3
  0.7 0.5 broadcast.25
  1.2 0.1 copy-done.3
  1.3 0.7 reduce.5
  2.0 0.1 reshape.38
  2.0 0.0 copy-start.4
  2.1 0.7 copy-done.4
  2.7 0.0 copy-start.5
  2.7 0.1 reshape.37
  2.8 0.6 copy-done.5
  3.4 0.0 copy-start.1
  3.4 0.0 copy-start.2
  3.4 0.6 copy.28.lengths
  4.0 0.0 copy-done.1
  4.0 0.0 copy-done.2
  4.0 0.6 fusion.9.my_small
  4.7 1.0 copy.27
  5.7 0.7 copy.35
  6.3 232.0 %run_layers.1 = (bf16[2,192,1024]{2,1,0:T(8,128)(2,1)}, f32[32,6272]{1,0:T(8,128)}) custom-call(s32[2,1]{1,0:T(2,128)} %copy.28.lengths, bf16[2,192,1024]{2,1,0:T(8,128)(2,1)} %bitcast.38, bf16[32,1536]{1,0:T(8,128)(2,1)} %bitcast.40, bf16[32,512]{1,0:T(8,128)(2,1)} %bitcast.43, bf16[32,2048]{1,0:T(8,128)(2,1)} %bitcast.41, bf16[32,2048]{1,0:T(8,128)(2,1)} %bitcast.42, ...), custom_call_target="tpu_custom_call" | custom-call | tf_op jit(solution)/shard_map/run_layers/pallas_call | solution.py:724
  238.3 0.9 slice_reduce_fusion
  239.2 0.7 reshape_squeeze.7
  239.9 0.8 slice_bitcast_fusion.4
  240.7 0.7 copy.30
  241.3 0.9 slice_bitcast_fusion.3
  242.2 0.1 copy.31
  242.3 0.6 reshape.41
  242.9 0.6 copy.29
  243.5 1.5 slice_bitcast_fusion.2
  245.0 0.9 slice.29
  245.9 0.0 copy-start
  245.9 1.9 slice_bitcast_fusion
  247.8 0.1 reshape.40
  248.0 0.7 copy.33
  248.7 0.0 copy-done
  248.7 0.9 copy.37
Async XLA Ops:
  0.6 0.7 copy-start.3
  2.0 0.7 copy-start.4
  2.7 0.7 copy-start.5
  3.4 0.7 copy-start.1
  3.4 0.7 copy-start.2
  245.9 2.8 %copy-start = (bf16[2,192,1024]{2,1,0:T(8,128)(2,1)S(1)}, bf16[2,192,1024]{2,1,0:T(8,128)(2,1)}, u32[]{:S(2)}) copy-start(bf16[2,192,1024]{2,1,0:T(8,128)(2,1)} %get-tuple-element.11) | copy-start | bytes 2359300

commit v3 on v2

--- a/solution.py
+++ b/solution.py
@@ -13,7 +13,14 @@
 BLOCK = 512
 EXTRA, UP, DOWN = 2048, 2176, 4224
 GATHERS = ((0, 2176, 1152), (UP, 2048, 1024), (DOWN, 2048, 1024))
-PASSES = ((DOWN, 2048, 1024), (UP, 2048, 1024), (0, 2176, 1152))
+PASSES = (
+    (DOWN, 1024, 512),
+    (DOWN + 1024, 1024, 512),
+    (UP, 1024, 512),
+    (UP + 1024, 1024, 512),
+    (0, 1536, 768),
+    (1536, 640, 384),
+)
 
 
 OFFSETS = (0, 3, 1, 2)
@@ -74,7 +81,7 @@
             copy.wait_send()
 
 
-N_EACH = 60
+N_EACH = 108
 N_GATHER = 147
 
 
@@ -125,7 +132,7 @@
 
 
 def layers_kernel(
-    lengths, ends, my_qkv, my_out, my_up, my_down, my_small,
+    lengths, ends, shard,
     ends_out, out,
     gains, shifts, b_qv, b_ff,
     d_gains, d_shifts, d_bqv, d_bff,
@@ -141,11 +148,8 @@
     own_load = pltpu.make_async_copy(ends.at[t], x_own, io_sems.at[0])
     own_load.start()
     own = blocks.at[t, x, y, c]
-    own[:, :, 0:1536] = my_qkv[...].reshape(2, 16, 1536)
-    own[:, :, 1536:EXTRA] = my_out[...].reshape(2, 16, 512)
-    own[:, :, EXTRA:UP] = low(my_small[...].T)[0:32].reshape(2, 16, 128)
-    own[:, :, UP:DOWN] = my_up[...].reshape(2, 16, 2048)
-    own[:, :, DOWN:COLS] = my_down[...].reshape(2, 16, 2048)
+    shard_load = pltpu.make_async_copy(shard, own, io_sems.at[1])
+    shard_load.start()
     meet(x, y, c, t)
     send = Sender(send_sems, recv_sems)
     share = Sender(gather_send_sems, gather_recv_sems)
@@ -252,7 +256,7 @@
 
     length = lengths[t, 0]
     first_half = lax.broadcasted_iota(jnp.int32, (ROWS, 128), 1) < HD
-    valid = lax.broadcasted_iota(jnp.int32, (ROWS, ROWS), 1) < length
+    valid = lax.broadcasted_iota(jnp.int32, (ROWS, ROWS), 0) < length
     scale = HD**-0.5
 
     def pick(e, value):
@@ -282,18 +286,17 @@
 
         def heads(i):
             at = columns(i * 128, 128)
-            kp, vp, qp = k[:, at], v[:, at], q[:, at]
-            outs = []
+            kp, vp, qp = k[:, at], v[:, at], q[:, at] * scale
+            vt, outs = vp.T, []
             for e in (0, 1):
-                scores = dot_nt(pick(e, qp), kp) * scale
-                scores = jnp.where(valid, scores, -1e9)
-                powers = jnp.exp(scores - jnp.max(scores, -1, keepdims=True))
-                p = low(powers / jnp.sum(powers, -1, keepdims=True))
+                scores = jnp.where(valid, dot_nt(kp, pick(e, qp)), -1e9)
+                powers = jnp.exp(scores - jnp.max(scores, 0, keepdims=True))
+                p = low(powers * (1.0 / total(powers)))
                 probs[2 * i + e] = p
-                outs.append(dot(p, vp))
-            o[:, at] = low(jnp.where(first_half, outs[0], outs[1]))
-
-        each(8, heads)
+                outs.append(dot(vt[64 * e : 64 * e + 64], p))
+            o[:, at] = low(jnp.concatenate(outs)).T
+
+        each(4, lambda i: (heads(2 * i), heads(2 * i + 1)))
         after("heads")
         attended = dot_nt(o[:, 0:512], w[0, :, 1536:2048]) + dot_nt(o[:, 512:1024], w[1, :, 1536:2048])
         normed, inverse = normalize(high(x[...]) + attended + shifts[0:1])
@@ -363,27 +366,30 @@
         res[...] = d_sum
         a_low[...] = low(d_sum)
         after("a_low")
+        for half in (0, 1):
+            d_qkv[2, :, half * 512 : half * 512 + 512] = low(dot(a_low[...], w[half, :, 1536:EXTRA]))
 
         def heads(i):
             at = columns(i * 128, 128)
-            half = lax.div(i, 4)
-            d_o = low(dot(a_low[...], w[half, :, columns(1536 + lax.rem(i, 4) * 128, 128)]))
-            kp, vp, qp = k[:, at], v[:, at], q[:, at]
-            parts = []
+            kp, vp, qp, d_o = k[:, at], v[:, at], q[:, at], d_qkv[2, :, at]
+            kt, parts = kp.T, []
             for e in (0, 1):
                 p_low = probs[2 * i + e]
                 p = high(p_low)
-                d_p = dot_nt(pick(e, d_o), vp)
-                d_s = low(p * (d_p - jnp.sum(p * d_p, -1, keepdims=True)))
-                parts.append((dot(d_s, kp) * scale, dot_tn(d_s, qp) * scale, dot_tn(p_low, d_o)))
-            d_q, d_k, d_v = (low(jnp.where(first_half, a, b)) for a, b in zip(*parts))
+                product = p * dot_nt(vp, pick(e, d_o))
+                d_s = low(product - p * total(product))
+                parts.append(
+                    (dot(kt[64 * e : 64 * e + 64], d_s) * scale, dot(d_s, qp) * scale, dot(p_low, d_o))
+                )
+            d_q = low(jnp.concatenate([parts[0][0], parts[1][0]])).T
+            d_k, d_v = (low(jnp.where(first_half, a, b)) for a, b in zip(parts[0][1:], parts[1][1:]))
             d_qkv[0, :, at] = d_q
             d_qkv[1, :, at] = d_k
             d_qkv[2, :, at] = d_v
             d_bqv[0:1, at] = total(high(d_q))
             d_bqv[1:2, at] = total(high(d_v))
 
-        each(8, heads)
+        each(4, lambda i: (heads(2 * i), heads(2 * i + 1)))
         after("d_qkv")
 
         def narrow_in(i):
@@ -409,30 +415,28 @@
             given[name].wait_recv()
 
     def block(start, left, right, s_left, s_right):
-        whole = low(dot_tn(left, right) + dot_tn(s_left, s_right))
+        whole = low(dot_tn(jnp.concatenate([left, s_left]), jnp.concatenate([right, s_right])))
         for chip in range(16):
             for h in (0, 1):
                 f, g = (chip // 4, chip % 4) if h == 0 else (chip % 4, chip // 4)
                 to, of = h * 512 + f * 128 + g * 32, chip * 64 + h * 32
                 w[0, to : to + 32, columns(start, right.shape[1])] = whole[of : of + 32]
 
-    def grads_down():
-        have("act", "d_low")
-
+    def grads_down(first):
         def one(i):
+            i = i + first
             at = columns(i * BLOCK, BLOCK)
             block(DOWN + i * BLOCK, d_low[...], act[:, columns(c * 2048 + i * BLOCK, BLOCK)], s_d_low[...], s_act[:, at])
 
-        each(4, one)
-
-    def grads_up():
-        have("hid", "d_act")
-
+        each(2, one)
+
+    def grads_up(first):
         def one(i):
+            i = i + first
             at = columns(i * BLOCK, BLOCK)
             block(UP + i * BLOCK, hid[...], d_act[:, columns(c * 2048 + i * BLOCK, BLOCK)], s_hid[...], s_d_act[:, at])
 
-        each(4, one)
+        each(2, one)
 
     def spread(row, size, offset):
         lanes = row.shape[1]
@@ -468,11 +472,12 @@
         dst[7:8] = spread(d_bff[:, units_at], 64, 0)
         dst[8:9] = spread(d_bff[:, units_at], 64, 32)
 
-    def grads_rest():
-        have("o", "a_low", "x", "d_qkv", "small")
-        block(1536, a_low[...], o[:, columns(c * 512, 512)], s_a_low[...], s_o[...])
+    def grads_qkv():
         for j in (0, 1, 2):
             block(j * 512, x_in[...], d_qkv[j, :, columns(c * 512, 512)], s_x[...], s_d_qkv[j])
+
+    def grads_rest():
+        block(1536, a_low[...], o[:, columns(c * 512, 512)], s_a_low[...], s_o[...])
         summed = small[0] + s_small[...]
         column = low(jnp.concatenate([summed, jnp.zeros((112, 1024), jnp.float32)], axis=0).T)
         for chip in range(16):
@@ -578,7 +583,7 @@
 
     def hand(n):
         whole, _, _ = parts(n)
-        handing[n] = remote(6 + n, to_mate.at[:, whole], out.at[:, whole], sibling)
+        handing[n] = remote(12 + n, to_mate.at[:, whole], out.at[:, whole], sibling)
 
         @pl.when(owner)
         def _():
@@ -606,18 +611,29 @@
             swap("d_low", d_low, s_d_low)
         if stage == "d_act":
             swap("d_act", d_act.at[:, other_half], s_d_act)
-            grads_down()
+            have("act", "d_low")
+            grads_down(0)
             far(0)
+            grads_down(2)
+            far(1)
         if stage == "a_low":
             swap("a_low", a_low, s_a_low)
-            grads_up()
-            far(1)
             near(0)
+            have("hid", "d_act")
+            grads_up(0)
+            far(2)
+            near(1)
+            grads_up(2)
+            far(3)
+            near(2)
         if stage == "d_qkv":
             swap("d_qkv", d_qkv.at[:, :, other_heads], s_d_qkv)
             small_rows(1 - c, small.at[1])
             swap("small", small.at[1], s_small)
-            near(1)
+            small_rows(c, small.at[0])
+            q_far(0)
+            near(3)
+            q_far(1)
 
     def first_stage(stage):
         if stage == "qkv":
@@ -638,6 +654,7 @@
             second_end(2, 1)
             complete(2)
 
+    shard_load.wait()
     z_sends = []
     for n, (start, size, _) in enumerate(GATHERS):
         part = own.at[:, :, pl.ds(start, size)]
@@ -681,23 +698,36 @@
     across = send(kept.at[2], ends_out.at[t], {"tensor": 1 - t})
     here = pltpu.make_async_copy(kept.at[2], ends_out.at[t], io_sems.at[1])
     here.start()
-    small_rows(c, small.at[0])
+    have("o", "a_low", "x", "d_qkv", "small")
+    grads_qkv()
+    far(4)
+    q_far(2)
+    q_near(0)
     grads_rest()
-    far(2)
-    q_far(0)
-    near(2)
-    q_far(1)
-    q_near(0)
+    far(5)
+    near(4)
     q_near(1)
+    q_far(3)
     cross(0)
-    q_far(2)
+    q_near(2)
     cross(1)
+    near(5)
+    q_near(3)
     hand(0)
-    q_near(2)
+    cross(2)
     hand(1)
-    cross(2)
+    q_far(4)
+    cross(3)
+    q_far(5)
     hand(2)
-    for n in (0, 1, 2):
+    q_near(4)
+    q_near(5)
+    hand(3)
+    cross(4)
+    cross(5)
+    hand(4)
+    hand(5)
+    for n in range(6):
 
         @pl.when(sender)
         def _():
@@ -714,7 +744,7 @@
     send.finish()
 
 
-def run_layers(lengths, ends, *shards):
+def run_layers(lengths, ends, shard):
     vmem = pltpu.VMEM
     bf, f32 = jnp.bfloat16, jnp.float32
     hbm = pl.BlockSpec(memory_space=pl.ANY)
@@ -727,7 +757,7 @@
             shape((2, ROWS, 1024), bf),
             shape((32, COLS), f32),
         ),
-        in_specs=[pl.BlockSpec(memory_space=pltpu.SMEM), hbm, near, near, near, near, near],
+        in_specs=[pl.BlockSpec(memory_space=pltpu.SMEM), hbm, hbm],
         out_specs=(hbm, near),
         scratch_shapes=[
             vmem((2, 1024), f32),
@@ -780,8 +810,8 @@
             vmem((2, 32, COLS), bf),
             vmem((32, COLS), f32),
             sem((2,)),
-            sem((N_EACH + 9,)),
-            sem((N_EACH + 9,)),
+            sem((N_EACH + 18,)),
+            sem((N_EACH + 18,)),
             sem((N_GATHER,)),
             sem((N_GATHER,)),
         ],
@@ -789,37 +819,79 @@
             collective_id=0, has_side_effects=True, vmem_limit_bytes=62 * 2**20
         ),
         name="run_layers",
-    )(lengths, ends, *shards)
+    )(lengths, ends, shard)
+
+
+def pack_kernel(w_qkv, w_out, w_up, w_down, gains, shifts, b_qv, b_ff, shard, small):
+    for j in (0, 1, 2):
+        shard[:, j * 512 : j * 512 + 512] = w_qkv[0, j]
+    shard[:, 1536:EXTRA] = w_out[0]
+    shard[:, UP:DOWN] = w_up[0]
+    shard[:, DOWN:COLS] = w_down[0]
+    small[...] = jnp.zeros_like(small)
+    small[0:2, 0:32] = high(gains[0])
+    small[2:6, 0:32] = high(shifts[0])
+    small[6:7, 0:32] = jnp.concatenate([high(b_qv[0, 0, 0:1]), high(b_qv[0, 0, 1:2])], axis=1)
+    small[7:8, 0:32] = high(b_ff[0, :, 0:32])
+    small[8:9, 0:32] = high(b_ff[0, :, 32:64])
+    shard[:, EXTRA:UP] = low(small[...].T[0:32])
 
 
 def pack_shard(w_qkv, w_out, w_up, w_down, gains, shifts, b_qv, b_ff):
-    small = jnp.concatenate([gains[0], shifts[0], b_qv.reshape(1, 32), b_ff.reshape(2, 32)], axis=0)
+    return pl.pallas_call(
+        pack_kernel,
+        out_shape=jax.ShapeDtypeStruct((32, COLS), jnp.bfloat16),
+        scratch_shapes=[pltpu.VMEM((128, 128), jnp.float32)],
+        name="pack_shard",
+    )(
+        w_qkv.transpose(0, 2, 1, 3),
+        w_out.transpose(0, 2, 1),
+        w_up,
+        w_down.transpose(0, 2, 1),
+        gains,
+        shifts,
+        b_qv.transpose(0, 2, 1, 3),
+        b_ff,
+    )
+
+
+def unpack_kernel(got, w_qkv, w_out, w_up, w_down, gains, shifts, b_qv, b_ff):
+    for j in (0, 1, 2):
+        w_qkv[0, j] = got[:, j * 512 : j * 512 + 512]
+    w_out[0] = got[:, 1536:EXTRA]
+    w_up[0] = got[:, UP:DOWN]
+    w_down[0] = got[:, DOWN:COLS]
+    rows = got[:, EXTRA:UP].T
+    gains[0] = rows[0:2]
+    shifts[0] = rows[2:6]
+    b_qv[0, 0, 0:1] = rows[6:7, 0:16]
+    b_qv[0, 0, 1:2] = rows[6:7, 16:32]
+    b_ff[0] = jnp.concatenate([rows[7:8], rows[8:9]], axis=1)
+
+
+def unpack_shard(got):
+    shapes = ((1, 3, 32, 512), (1, 32, 512), (1, 32, 2048), (1, 32, 2048), (1, 2, 32), (1, 4, 32))
+    shapes = shapes + ((1, 1, 2, 16), (1, 1, 64))
+    w_qkv, w_out, w_up, w_down, gains, shifts, b_qv, b_ff = pl.pallas_call(
+        unpack_kernel,
+        out_shape=tuple(jax.ShapeDtypeStruct(shape, jnp.float32) for shape in shapes),
+        name="unpack_shard",
+    )(got)
     return (
-        w_qkv[0].reshape(32, 1536),
-        w_out[0].T,
-        w_up[0],
-        w_down[0].T,
-        jnp.pad(small.astype(jnp.float32), ((0, 119), (0, 96))),
+        w_qkv.transpose(0, 2, 1, 3),
+        w_out.transpose(0, 2, 1),
+        w_up,
+        w_down.transpose(0, 2, 1),
+        gains,
+        shifts,
+        b_qv.transpose(0, 2, 1, 3),
+        b_ff,
     )
 
 
-def unpack_shard(got):
-    extra = got[:, EXTRA:UP]
-    return (
-        got[:, :1536].reshape(1, 32, 3, 512),
-        got[:, 1536:2048].T[None],
-        got[:, UP:DOWN][None],
-        got[:, DOWN:].T[None],
-        extra[:, 0:2].T[None],
-        extra[:, 2:6].T[None],
-        extra[:, 6].reshape(1, 2, 1, 16),
-        extra[:, 7:9].T.reshape(1, 1, 64),
-    )
-
-
-def body(ends, lengths, w_qkv, w_out, w_up, w_down, gains, shifts, b_qv, b_ff):
-    shards = pack_shard(w_qkv, w_out, w_up, w_down, gains, shifts, b_qv, b_ff)
-    ends_out, got = run_layers(lengths, ends.reshape(2, ROWS, 1024), *shards)
+def body(ends, lengths, *weights):
+    shard = pack_shard(*weights)
+    ends_out, got = run_layers(lengths, ends.reshape(2, ROWS, 1024), shard.reshape(2, 16, COLS))
     return (ends_out.reshape(1, 2, 1, ROWS, 1024),) + unpack_shard(got)
 
 

time: 250 us -> 231 us (0.924)
  local copies, waits for them, and re-layouts: 15.6 us -> 2.18 us
  Pallas kernels: 232 us -> 228 us
    pallas_call x1, Pallas kernels: 232 us -> 224 us  [run_layers(): pl.pallas_call(layers_kernel, out_shape=(shape((2, ROWS, 1024), bf), shap...]
    pallas_call x0 -> x2, Pallas kernels: none -> 4.1 us  [the longest x1 2.15 us: unpack_shard(): pl.pallas_call(unpack_kernel, out_shape=tuple((jax.ShapeDtypeStruct(shape...]
    unnamed x18 -> x6, local copies, waits for them, and re-layouts: 5.82 us -> 2.18 us
    broadcast_in_dim x2 -> x0, local copies, waits for them, and re-layouts: 3.4 us -> none  [the longest x1 1.93 us: unpack_shard(): got[:, DOWN:].T[None]]
    transpose x5 -> x0, local copies, waits for them, and re-layouts: 3.02 us -> none  [the longest x2 1.44 us: unpack_shard(): extra[:, 2:6].T[None]]
where the time goes in v3:
time: 231 us
  Pallas kernels  228 us (99%)
    pallas_call x1, Pallas kernels, run_layers(): pl.pallas_call(layers_kernel, out_shape=(shape((2, ROWS, 1024), bf), shap...  224 us

profile of v3, /device:TPU:1, one launch (start us, length us, event | category | flops | bytes accessed | tf_op | source)
XLA Modules:
  0.0 231.0 jit_solution(12317913969958392261)
XLA Ops:
  0.6 0.0 copy-start.1
  0.7 0.6 copy-done.1
  1.3 0.6 copy.19.lengths
  1.9 2.0 pack_shard.1
  3.9 224.1 %run_layers.1 = (bf16[2,192,1024]{2,1,0:T(8,128)(2,1)}, f32[32,6272]{1,0:T(8,128)}) custom-call(s32[2,1]{1,0:T(2,128)} %copy.19.lengths, bf16[2,192,1024]{2,1,0:T(8,128)(2,1)} %bitcast.17, bf16[2,16,6272]{2,1,0:T(8,128)(2,1)} %bitcast.15), custom_call_target="tpu_custom_call" | custom-call | tf_op jit(solution)/shard_map/run_layers/pallas_call | solution.py:754
  228.0 0.0 copy-start
  228.0 2.1 unpack_shard.1
  230.1 0.0 copy-done
  230.1 0.9 copy.23
Async XLA Ops:
  0.6 0.7 copy-start.1
  228.0 2.2 copy-start

commit v4 on v3

--- a/solution.py
+++ b/solution.py
@@ -51,7 +51,8 @@
         {"dp": dp_at(x, lax.rem(y + 3, 4), c)},
         {"dp": dp_at(x, y, 1 - c)},
         {"tensor": 1 - t},
-        {"section": 1 - lax.axis_index("section")},
+        {"dp": dp_at(x, y, 1 - c), "tensor": 1 - t},
+        {"section": 1 - lax.axis_index("section"), "dp": dp_at(x, y, t), "tensor": c},
     ]
     for partner in partners:
         pl.semaphore_signal(barrier, inc=1, device_id=partner, device_id_type=MESH)
@@ -81,7 +82,7 @@
             copy.wait_send()
 
 
-N_EACH = 108
+N_EACH = 107
 N_GATHER = 147
 
 
@@ -132,14 +133,14 @@
 
 
 def layers_kernel(
-    lengths, ends, shard,
+    spans, ends, shard,
     ends_out, out,
     gains, shifts, b_qv, b_ff,
     d_gains, d_shifts, d_bqv, d_bff,
     blocks, x_own, x_in, relay, q, k, v, o, probs, n1, n2, i1, i2, res, hid, act, slope, d_act, d_qkv,
     acc, d_low, a_low, kept, small,
     s_x, s_hid, s_d_low, s_a_low, s_act, s_d_act, s_o, s_d_qkv, s_small,
-    passing, near_p, near_m, q_passing, q_p, q_m, mate, to_mate,
+    passing, near_p, near_m, q_passing, q_p, q_m, mate, to_mate, span, span_in,
     io_sems, send_sems, recv_sems, gather_send_sems, gather_recv_sems,
 ):
     x, y, c, t = place()
@@ -254,9 +255,8 @@
                 shifts[...] = rows[2:6]
             collect(half, (rows[6:7], rows[7:8], rows[8:9]))
 
-    length = lengths[t, 0]
     first_half = lax.broadcasted_iota(jnp.int32, (ROWS, 128), 1) < HD
-    valid = lax.broadcasted_iota(jnp.int32, (ROWS, ROWS), 0) < length
+    position = lax.broadcasted_iota(jnp.int32, (ROWS, ROWS), 0).astype(jnp.float32)
     scale = HD**-0.5
 
     def pick(e, value):
@@ -289,7 +289,7 @@
             kp, vp, qp = k[:, at], v[:, at], q[:, at] * scale
             vt, outs = vp.T, []
             for e in (0, 1):
-                scores = jnp.where(valid, dot_nt(kp, pick(e, qp)), -1e9)
+                scores = jnp.where(position < span[0:1, 0:1], dot_nt(kp, pick(e, qp)), -1e9)
                 powers = jnp.exp(scores - jnp.max(scores, 0, keepdims=True))
                 p = low(powers * (1.0 / total(powers)))
                 probs[2 * i + e] = p
@@ -602,7 +602,9 @@
             handing[n].start()
 
     def exchange(n):
-        copy = send(kept.at[n], relay.at[n], {"section": 1 - s})
+        copy = send(
+            kept.at[n], relay.at[n], {"section": 1 - s, "dp": dp_at(x, y, t), "tensor": c}
+        )
         copy.wait_recv()
         return relay[n]
 
@@ -654,6 +656,16 @@
             second_end(2, 1)
             complete(2)
 
+    lent = (
+        remote(18, ends.at[1 - t], x_in, sibling),
+        remote(19, spans.at[1 - t], span_in, sibling),
+    )
+
+    @pl.when(owner)
+    def _():
+        for copy in lent:
+            copy.start()
+
     shard_load.wait()
     z_sends = []
     for n, (start, size, _) in enumerate(GATHERS):
@@ -682,6 +694,15 @@
     complete(0)
     take_parameters()
     own_load.wait()
+    span[...] = spans[t]
+
+    @pl.when(sender)
+    def _():
+        for copy in lent:
+            copy.wait_recv()
+        x_own[...] = jnp.where(s == 1, x_in[...], x_own[...])
+        span[...] = jnp.where(s == 1, span_in[...], span[...])
+
     kept[0] = forward(x_own, first_stage)
     share.finish()
     x_in[...] = jnp.where(s == 0, x_own[...], exchange(0))
@@ -695,9 +716,23 @@
     grad_out = jnp.where(s == 1, x_own[...], exchange(1))
     d_x = backward(high(grad_out), last_stage)
     kept[2] = jnp.where(s == 0, d_x, kept[2])
-    across = send(kept.at[2], ends_out.at[t], {"tensor": 1 - t})
-    here = pltpu.make_async_copy(kept.at[2], ends_out.at[t], io_sems.at[1])
-    here.start()
+    slot = t + s * (c - t)
+    done, moved = kept.at[2], (s == 1) & sender
+    here = pltpu.make_async_copy(done, ends_out.at[slot], io_sems.at[1])
+    beyond = remote(20, done, ends_out.at[slot], {"tensor": 1 - t})
+    to_core = remote(21, done, ends_out.at[slot], sibling)
+    to_cross = remote(22, done, ends_out.at[slot], {"dp": dp_at(x, y, 1 - c), "tensor": 1 - t})
+
+    @pl.when(moved)
+    def _():
+        to_core.start()
+        to_cross.start()
+
+    @pl.when(jnp.logical_not(moved))
+    def _():
+        here.start()
+        beyond.start()
+
     have("o", "a_low", "x", "d_qkv", "small")
     grads_qkv()
     far(4)
@@ -739,12 +774,34 @@
         def _():
             handing[n].wait_send()
 
-    here.wait()
-    across.wait_recv()
+    @pl.when(moved)
+    def _():
+        to_core.wait_send()
+        to_cross.wait()
+        beyond.wait_recv()
+
+    @pl.when(jnp.logical_not(moved))
+    def _():
+        here.wait()
+        beyond.wait_send()
+
+    @pl.when(s == 0)
+    def _():
+        beyond.wait_recv()
+
+    @pl.when((s == 1) & owner)
+    def _():
+        to_core.wait_recv()
+
+    @pl.when(owner)
+    def _():
+        for copy in lent:
+            copy.wait_send()
+
     send.finish()
 
 
-def run_layers(lengths, ends, shard):
+def run_layers(spans, ends, shard):
     vmem = pltpu.VMEM
     bf, f32 = jnp.bfloat16, jnp.float32
     hbm = pl.BlockSpec(memory_space=pl.ANY)
@@ -757,7 +814,7 @@
             shape((2, ROWS, 1024), bf),
             shape((32, COLS), f32),
         ),
-        in_specs=[pl.BlockSpec(memory_space=pltpu.SMEM), hbm, hbm],
+        in_specs=[near, hbm, hbm],
         out_specs=(hbm, near),
         scratch_shapes=[
             vmem((2, 1024), f32),
@@ -809,9 +866,11 @@
             vmem((2, 32, COLS), bf),
             vmem((2, 32, COLS), bf),
             vmem((32, COLS), f32),
+            vmem((8, 128), f32),
+            vmem((8, 128), f32),
             sem((2,)),
-            sem((N_EACH + 18,)),
-            sem((N_EACH + 18,)),
+            sem((N_EACH + 23,)),
+            sem((N_EACH + 23,)),
             sem((N_GATHER,)),
             sem((N_GATHER,)),
         ],
@@ -819,7 +878,7 @@
             collective_id=0, has_side_effects=True, vmem_limit_bytes=62 * 2**20
         ),
         name="run_layers",
-    )(lengths, ends, shard)
+    )(spans, ends, shard)
 
 
 def pack_kernel(w_qkv, w_out, w_up, w_down, gains, shifts, b_qv, b_ff, shard, small):
@@ -891,7 +950,8 @@
 
 def body(ends, lengths, *weights):
     shard = pack_shard(*weights)
-    ends_out, got = run_layers(lengths, ends.reshape(2, ROWS, 1024), shard.reshape(2, 16, COLS))
+    spans = jnp.broadcast_to(lengths[:, :, None].astype(jnp.float32), (2, 8, 128))
+    ends_out, got = run_layers(spans, ends.reshape(2, ROWS, 1024), shard.reshape(2, 16, COLS))
     return (ends_out.reshape(1, 2, 1, ROWS, 1024),) + unpack_shard(got)
 
 

time: 231 us -> 224 us (0.970)
  Pallas kernels: 228 us -> 221 us
    pallas_call x1, Pallas kernels: 224 us -> 217 us  [run_layers(): pl.pallas_call(layers_kernel, out_shape=(shape((2, ROWS, 1024), bf), shap...]
where the time goes in v4:
time: 224 us
  Pallas kernels  221 us (99%)
    pallas_call x1, Pallas kernels, run_layers(): pl.pallas_call(layers_kernel, out_shape=(shape((2, ROWS, 1024), bf), shap...  217 us

profile of v4, /device:TPU:1, one launch (start us, length us, event | category | flops | bytes accessed | tf_op | source)
XLA Modules:
  0.0 223.7 jit_solution(2982581604554382986)
XLA Ops:
  0.6 0.0 copy-start.1
  0.7 0.6 copy-done.1
  1.3 0.7 broadcast_in_dim.2.spans
  2.0 2.0 pack_shard.1
  3.9 216.7 %run_layers.1 = (bf16[2,192,1024]{2,1,0:T(8,128)(2,1)}, f32[32,6272]{1,0:T(8,128)}) custom-call(f32[2,8,128]{2,1,0:T(8,128)} %broadcast_in_dim.2.spans, bf16[2,192,1024]{2,1,0:T(8,128)(2,1)} %bitcast.18, bf16[2,16,6272]{2,1,0:T(8,128)(2,1)} %bitcast.17), custom_call_target="tpu_custom_call" | custom-call | tf_op jit(solution)/shard_map/run_layers/pallas_call | solution.py:811
  220.6 0.0 copy-start
  220.6 2.1 unpack_shard.1
  222.8 0.0 copy-done
  222.8 0.9 copy.22
  (1 shorter events, 0.0 us)
Async XLA Ops:
  0.6 0.7 copy-start.1
  220.6 2.2 copy-start

commit v5 on v4

--- a/solution.py
+++ b/solution.py
@@ -281,7 +281,7 @@
             def _():
                 v[:, at] = low(p + b_qv[1:2, at])
 
-        each(6, project)
+        each(3, lambda i: (project(2 * i), project(2 * i + 1)))
         after("qkv")
 
         def heads(i):
@@ -296,7 +296,7 @@
                 outs.append(dot(vt[64 * e : 64 * e + 64], p))
             o[:, at] = low(jnp.concatenate(outs)).T
 
-        each(4, lambda i: (heads(2 * i), heads(2 * i + 1)))
+        each(2, lambda i: [heads(4 * i + u) for u in range(4)])
         after("heads")
         attended = dot_nt(o[:, 0:512], w[0, :, 1536:2048]) + dot_nt(o[:, 512:1024], w[1, :, 1536:2048])
         normed, inverse = normalize(high(x[...]) + attended + shifts[0:1])
@@ -314,7 +314,7 @@
             act[:, at] = low(u * phi)
             slope[:, at] = low(phi + u * (jnp.exp(u * u * -0.5) * 0.3989422804014327))
 
-        each(8, widen)
+        each(4, lambda i: (widen(2 * i), widen(2 * i + 1)))
         after("act")
 
         def narrow(i):
@@ -324,7 +324,7 @@
                 act[:, 2048:4096], w[1, rows, DOWN:COLS]
             )
 
-        each(4, narrow)
+        each(2, lambda i: (narrow(2 * i), narrow(2 * i + 1)))
         normed, inverse = normalize(res[...] + acc[...] + shifts[2:3])
         n2[...], i2[...] = normed, inverse
         return low(normed * gains[1:2] + shifts[3:4])
@@ -346,7 +346,7 @@
             d_act[:, at] = d
             d_bff[:, at] = total(high(d))
 
-        each(8, widen)
+        each(4, lambda i: (widen(2 * i), widen(2 * i + 1)))
         after("d_act")
 
         def narrow(i):
@@ -356,7 +356,7 @@
                 d_act[:, 2048:4096], w[1, rows, UP:DOWN]
             )
 
-        each(4, narrow)
+        each(2, lambda i: (narrow(2 * i), narrow(2 * i + 1)))
         d_hidden = res[...] + acc[...]
         normed = n1[...]
         d_gains[0:1] = total(d_hidden * normed)
@@ -389,7 +389,7 @@
             d_bqv[0:1, at] = total(high(d_q))
             d_bqv[1:2, at] = total(high(d_v))
 
-        each(4, lambda i: (heads(2 * i), heads(2 * i + 1)))
+        each(2, lambda i: [heads(4 * i + u) for u in range(4)])
         after("d_qkv")
 
         def narrow_in(i):
@@ -401,7 +401,7 @@
                 for j in (0, 1, 2)
             )
 
-        each(4, narrow_in)
+        each(2, lambda i: (narrow_in(2 * i), narrow_in(2 * i + 1)))
         return low(res[...] + acc[...])
 
     other_half = columns((1 - c) * 2048, 2048)
@@ -428,7 +428,8 @@
             at = columns(i * BLOCK, BLOCK)
             block(DOWN + i * BLOCK, d_low[...], act[:, columns(c * 2048 + i * BLOCK, BLOCK)], s_d_low[...], s_act[:, at])
 
-        each(2, one)
+        one(0)
+        one(1)
 
     def grads_up(first):
         def one(i):
@@ -436,7 +437,8 @@
             at = columns(i * BLOCK, BLOCK)
             block(UP + i * BLOCK, hid[...], d_act[:, columns(c * 2048 + i * BLOCK, BLOCK)], s_hid[...], s_d_act[:, at])
 
-        each(2, one)
+        one(0)
+        one(1)
 
     def spread(row, size, offset):
         lanes = row.shape[1]

time: 224 us -> 220 us (0.982)
  Pallas kernels: 221 us -> 217 us
    pallas_call x1, Pallas kernels: 217 us -> 213 us  [run_layers(): pl.pallas_call(layers_kernel, out_shape=(shape((2, ROWS, 1024), bf), shap...]
where the time goes in v5:
time: 220 us
  Pallas kernels  217 us (99%)
  local copies, waits for them, and re-layouts  2.21 us (1%)
    pallas_call x1, Pallas kernels, run_layers(): pl.pallas_call(layers_kernel, out_shape=(shape((2, ROWS, 1024), bf), shap...  213 us

profile of v5, /device:TPU:1, one launch (start us, length us, event | category | flops | bytes accessed | tf_op | source)
XLA Modules:
  0.0 219.7 jit_solution(17001252338422958258)
XLA Ops:
  0.6 0.0 copy-start.1
  0.7 0.6 copy-done.1
  1.3 0.7 broadcast_in_dim.2.spans
  2.0 2.0 pack_shard.1
  3.9 212.7 %run_layers.1 = (bf16[2,192,1024]{2,1,0:T(8,128)(2,1)}, f32[32,6272]{1,0:T(8,128)}) custom-call(f32[2,8,128]{2,1,0:T(8,128)} %broadcast_in_dim.2.spans, bf16[2,192,1024]{2,1,0:T(8,128)(2,1)} %bitcast.18, bf16[2,16,6272]{2,1,0:T(8,128)(2,1)} %bitcast.17), custom_call_target="tpu_custom_call" | custom-call | tf_op jit(solution)/shard_map/run_layers/pallas_call | solution.py:813
  216.7 0.0 copy-start
  216.7 2.1 unpack_shard.1
  218.8 0.0 copy-done
  218.8 0.9 copy.22
  (1 shorter events, 0.0 us)
Async XLA Ops:
  0.6 0.7 copy-start.1
  216.7 2.2 copy-start
